TPU v7x, 1024 devices: a whole 4x8x16 slice. The times are simulated.
1024 devices in a mesh: row: 4 (over x), pitch: 64 (over y, z_lo), span: 4 (over z_hi, core).
Axes of the slice: x: 4, y: 8, z: 16 (z_hi: 2, z_lo: 8; z = z_hi * 8 + z_lo), core: 2. Of those that a mesh axis runs over, the one named last changes fastest.
Arguments:
- unknowns_array: float32 [4, 11, 5, 2048, 512], P('row', None, None, 'pitch', 'span'), may hold values from -6 to 6
- exit_spec: float32 [4, 2, 5, 5, 512], P('row', None, None, None, 'span'), may hold values from -4 to 4
- blades: int32 [4], replicated, may hold values from 24 to 96
- harmonics: int32 [4, 5], replicated, may hold values from 1 to 8
- pitch_jac: float32 [5, 5], replicated, may hold values from -2.5 to 2.5
- span_jac: float32 [5, 5], replicated, may hold values from -2.5 to 2.5
- send_cell: int32 [4, 4, 64, 256], P('row', 'span', 'pitch'), may hold values from 0 to 4095, as said below
- recv_order: int32 [4, 4, 64, 256], P('row', 'span', 'pitch'), may hold values from 0 to 255, each once within a row
Outputs:
- updated_unknowns: float32 [4, 11, 5, 2048, 512], P('row', None, None, 'pitch', 'span')
- surface_target_values: float32 [4, 4, 11, 5, 16384], P('row', 'span', None, None, 'pitch')
Inputs may be any that keep to these rules, and one draw needn't show every extreme that they name: `send_cell`: within each block of one row, one span index and one pitch index the 256 entries are distinct; entries k * 4 to (k + 1) * 4 - 1 are the cells whose wall values go to the solid block of pitch index k.
All inputs are finite; a program needn't handle non-finite values.
Results may differ from a plain program's by a relative error of at most 0.0001.
Values sent between devices are 32-bit elements; how exact they have to be, the bound alone decides.
A program may use at most 64 MiB of HBM per device.

v0:
```python
import math

import jax
import jax.numpy as jnp
from jax import lax
from jax.sharding import PartitionSpec as P

H = 5
SNAPSHOT_COUNT = 11
QUANTITY_COUNT = 5


full_turn = 2.0 * math.pi
step_size = 0.25
damping = 1.0 / 16.0
coupling = 0.5
frequency = 0.5
far_weight = 0.5


def from_root(value, axis, root):
    mine = lax.axis_index(axis) == root
    return lax.psum(jnp.where(mine, value, jnp.zeros_like(value)), axis)


def with_halo(value, sides, width, wrap):
    for axis, dim in sides:
        size, length = (lax.axis_size(axis), value.shape[dim])
        up = [(i, (i + 1) % size) for i in range(size if wrap else size - 1)]
        down = [(j, i) for i, j in up]
        last = lax.slice_in_dim(value, length - width, length, axis=dim)
        leading = lax.slice_in_dim(value, 0, width, axis=dim)
        before = lax.ppermute(last, axis, up)
        after = lax.ppermute(leading, axis, down)
        value = jnp.concatenate([before, value, after], axis=dim)
    return value


def fourier_derivative_operator(count):
    index_row = jnp.arange(count, dtype=jnp.int32)
    offset = (index_row[:, None] - index_row[None, :]).astype(jnp.float32)
    nonzero = jnp.where(offset == 0, 1.0, offset)
    entries = 0.5 * frequency * jnp.cos(math.pi * offset) / jnp.sin(math.pi * nonzero / count)
    return jnp.where(offset == 0, 0.0, entries)


def interface_values(
    spectrum, airfoil_number, spectral_cascade_update, angular_point_number, angular_width_whole
):
    snapshot_moments = jnp.arange(SNAPSHOT_COUNT, dtype=jnp.int32)
    airfoil_cycle_duration = angular_width_whole * SNAPSHOT_COUNT
    angle_shift = (
        spectral_cascade_update[None, None, :]
        * airfoil_number
        * angular_point_number[None, :, None]
        * SNAPSHOT_COUNT
        + spectral_cascade_update[None, None, :]
        * snapshot_moments[:, None, None]
        * angular_width_whole
    ) % airfoil_cycle_duration
    angle = angle_shift.astype(jnp.float32) * (full_turn / airfoil_cycle_duration)
    table = jnp.concatenate([jnp.cos(angle), jnp.sin(angle)], axis=2)
    coeffs = spectrum.reshape(2 * H, spectrum.shape[2], spectrum.shape[3])
    return jnp.einsum("tjk,kcs->tcjs", table, coeffs, precision=lax.Precision.HIGHEST)


def advance(solution_array, pitch_ext, span_ext, heard, pitch_jac, span_jac):
    pitch_first = 0.5 * (pitch_ext[:, :, 3:-1] - pitch_ext[:, :, 1:-3])
    pitch_fourth = (
        pitch_ext[:, :, 4:]
        - 4.0 * pitch_ext[:, :, 3:-1]
        + 6.0 * solution_array
        - 4.0 * pitch_ext[:, :, 1:-3]
        + pitch_ext[:, :, :-4]
    )
    span_first = 0.5 * (span_ext[..., 3:-1] - span_ext[..., 1:-3])
    span_fourth = (
        span_ext[..., 4:]
        - 4.0 * span_ext[..., 3:-1]
        + 6.0 * solution_array
        - 4.0 * span_ext[..., 1:-3]
        + span_ext[..., :-4]
    )
    flux = jnp.einsum("ac,tcjs->tajs", pitch_jac, pitch_first, precision=lax.Precision.HIGHEST)
    flux = flux + jnp.einsum("ac,tcjs->tajs", span_jac, span_first, precision=lax.Precision.HIGHEST)
    chronological_term = jnp.einsum(
        "ng,gwvy->nwvy",
        fourier_derivative_operator(SNAPSHOT_COUNT),
        solution_array,
        precision=lax.Precision.HIGHEST,
    )
    change = (
        flux
        + damping * (pitch_fourth + span_fourth)
        + chronological_term
        + coupling * (2.0 * solution_array - heard)
    )
    return solution_array - step_size * change


def source_weight(source, row_index):
    distance = jnp.abs(source - row_index)
    return jnp.where(distance == 1, 1.0, jnp.where(distance >= 2, far_weight, 0.0)).astype(
        jnp.float32
    )


def local(unknowns_array, exit_spec, blades, harmonics, pitch_jac, span_jac, send_cell, recv_order):
    solution_array = unknowns_array[0]
    spectrum = exit_spec[0]
    angular_portion = solution_array.shape[2]
    radius_portion = solution_array.shape[3]
    angular_width_whole = angular_portion * lax.axis_size("pitch")
    angular_point_number = lax.axis_index("pitch") * angular_portion + jnp.arange(
        angular_portion, dtype=jnp.int32
    )
    row_index = lax.axis_index("row")
    row_count = lax.axis_size("row")
    heard = jnp.zeros_like(solution_array)
    for owner in range(row_count):
        received = from_root(spectrum, "row", owner)
        face = interface_values(
            received, blades[owner], harmonics[owner], angular_point_number, angular_width_whole
        )
        heard = heard + source_weight(owner, row_index) * face
    pitch_ext = with_halo(solution_array, (("pitch", 2),), 2, True)
    span_ext = with_halo(solution_array, (("span", 3),), 2, False)
    updated_solution = advance(solution_array, pitch_ext, span_ext, heard, pitch_jac, span_jac)
    linear_mesh_points = updated_solution.reshape(
        SNAPSHOT_COUNT, QUANTITY_COUNT, angular_portion * radius_portion
    )
    outgoing = jnp.take(linear_mesh_points, send_cell[0, 0, 0], axis=2)
    delivered_surface = lax.all_to_all(outgoing, "pitch", split_axis=2, concat_axis=2, tiled=True)
    positioned_surface = jnp.take(delivered_surface, recv_order[0, 0, 0], axis=2)
    return (updated_solution[None], positioned_surface[None, None])


def solution(mesh):
    return jax.shard_map(
        local,
        mesh=mesh,
        in_specs=(
            P("row", None, None, "pitch", "span"),
            P("row", None, None, None, "span"),
            P(),
            P(),
            P(),
            P(),
            P("row", "span", "pitch", None),
            P("row", "span", "pitch", None),
        ),
        out_specs=(P("row", None, None, "pitch", "span"), P("row", "span", None, None, "pitch")),
        check_vma=False,
    )
```

profile of v0, /device:TPU:1, one launch (start us, length us, event | category | flops | bytes accessed | tf_op | source)
XLA Modules:
  0.0 175.2 jit_solution(13673658365801206269)
XLA Ops:
  7.2 1.2 copy.132
  8.5 1.2 fusion.100
  9.7 1.7 copy.86
  11.4 16.1 %collective-permute-start.2 = (f32[11,5,32,2]{2,3,1,0:T(2,128)S(1)}, f32[11,5,32,2]{2,3,1,0:T(2,128)S(1)}, u32[]{:S(2)}, u32[]{:S(2)}) collective-permute-start(f32[11,5,32,2]{2,3,1,0:T(2,128)S(1)} %copy.86), channel_id=1, source_target_pairs={{1,0},{2,1},{3,2},{5,4},{6,5},{7,6},{9,8},{10,9},{11,10},{13,12},{... | collective-permute-start | bytes 42248 | tf_op jit(solution)/shard_map/ppermute | solution.py:34
  27.8 6.3 %collective-permute-start.3 = (f32[11,5,32,2]{2,3,1,0:T(2,128)S(1)}, f32[11,5,32,2]{2,3,1,0:T(2,128)S(1)}, u32[]{:S(2)}, u32[]{:S(2)}) collective-permute-start(f32[11,5,32,2]{2,3,1,0:T(2,128)S(1)} %copy.88), channel_id=1, source_target_pairs={{0,1},{1,2},{2,3},{4,5},{5,6},{6,7},{8,9},{9,10},{10,11},{12,13},{... | collective-permute-start | bytes 42248 | tf_op jit(solution)/shard_map/ppermute | solution.py:33
  34.2 11.7 %collective-permute-start = (f32[11,5,2,128]{3,2,0,1:T(2,128)S(1)}, f32[11,5,2,128]{3,2,0,1:T(2,128)S(1)}, u32[]{:S(2)}, u32[]{:S(2)}) collective-permute-start(f32[11,5,2,128]{3,2,0,1:T(2,128)S(1)} %get-tuple-element.18), channel_id=1, source_target_pairs={{4,0},{8,4},{12,8},{16,12},{20,16},{24,20},{28,24},{32,28},{36,32}... | collective-permute-start | bytes 168968 | tf_op jit(solution)/shard_map/ppermute | solution.py:34
  45.9 1.9 %collective-permute-start.1 = (f32[11,5,2,128]{3,2,0,1:T(2,128)S(1)}, f32[11,5,2,128]{3,2,0,1:T(2,128)S(1)}, u32[]{:S(2)}, u32[]{:S(2)}) collective-permute-start(f32[11,5,2,128]{3,2,0,1:T(2,128)S(1)} %get-tuple-element.19), channel_id=1, source_target_pairs={{0,4},{4,8},{8,12},{12,16},{16,20},{20,24},{24,28},{28,32},{32,36}... | collective-permute-start | bytes 168968 | tf_op jit(solution)/shard_map/ppermute | solution.py:33
  49.1 0.6 copy.96
  49.7 0.6 copy.98
  50.4 0.7 fusion.101
  51.1 2.7 %fusion.13 = f32[11,5,32,128]{3,0,2,1:T(8,128)} fusion(f32[11,5,32,128]{3,2,1,0:T(8,128)S(1)} %bitcast.114), kind=kOutput, calls=%fused_computation.23 | convolution fusion | flops 29738048 | bytes 1802240 | tf_op jit(solution)/shard_map/ng,gwvy->nwvy/dot_general | solution.py:86
  53.9 2.4 %broadcast_multiply_fusion = (s32[5]{0:T(128)S(1)}, s32[5]{0:T(128)S(1)}, s32[5]{0:T(128)S(1)}, s32[5]{0:T(128)S(1)}) fusion(s32[]{:T(128)} %bitcast.31, s32[4,5]{1,0:T(4,128)S(1)} %copy-done.8, s32[]{:T(128)} %bitcast.25, s32[]{:T(128)} %bitcast.19, s32[]{:T(128)} %bitcast.13), kind=kLoop, calls=%fused_computation.152 | loop fusion | flops 20 | bytes 176 | tf_op jit(solution)/shard_map/mul | solution.py:53
  58.4 1.1 collective-permute-done.1
  59.5 1.2 subtract_multiply_fusion.1
  60.7 2.9 %fusion = f32[11,32,128,5]{2,3,1,0:T(8,128)} fusion(f32[11,5,32,128]{3,2,0,1:T(8,128)S(1)} %get-tuple-element.17, f32[5,5]{1,0:T(8,128)S(1)} %copy-done), kind=kOutput, calls=%fused_computation.6 | convolution fusion | flops 13516800 | bytes 1802340 | tf_op jit(solution)/shard_map/ac,tcjs->tajs/dot_general | solution.py:85
  63.7 2.9 %fusion.2 = f32[11,32,128,5]{2,3,1,0:T(8,128)} fusion(f32[11,5,32,128]{3,2,0,1:T(8,128)S(1)} %get-tuple-element.16, f32[5,5]{1,0:T(8,128)S(1)} %copy-done.10), kind=kOutput, calls=%fused_computation.8 | convolution fusion | flops 13516800 | bytes 1802340 | tf_op jit(solution)/shard_map/ac,tcjs->tajs/dot_general | solution.py:84
  66.6 41.4 %all-reduce.3.cloned.1.call-done = (f32[10,5,128]{2,0,1:T(8,128)}, f32[10,5,128]{2,0,1:T(8,128)}, f32[10,5,128]{2,0,1:T(8,128)}, f32[10,5,128]{2,0,1:T(8,128)}) async-done(((f32[10,5,128]{2,0,1:T(8,128)}, f32[10,5,128]{2,0,1:T(8,128)}, f32[10,5,128]{2,0,1:T(8,128)}, f32[10,5,128]{2,0,1:T(8,128)}), (f32[10,5,128]{2,0,1:T(8,128)}, f32[10,5,128]{2,0,1:T(8,128)}, f32[10,5,128]{2,0,1:T(8,128)}, ...) | async-done | bytes 102416 | tf_op jit(solution)/shard_map/psum | solution.py:23
  108.0 1.7 convolution_multiply_fusion.3
  109.7 1.9 %fusion.12 = f32[5,128,11,32]{1,3,2,0:T(8,128)S(1)} fusion(f32[5,128,11,32]{1,3,2,0:T(8,128)S(1)} %convolution_multiply_fusion.3, f32[]{:T(128)S(6)} %select_n.145, f32[11,32,5]{1,2,0:T(8,128)S(1)} %get-tuple-element.31, f32[11,32,5]{1,2,0:T(8,128)S(1)} %get-tuple-element.30, f32[10,5,128]{2,0,1:T(8,128)} %get-tuple-element.13), kind=kOutput, calls=%fused_computation.21 | convolution fusion | flops 27487680 | bytes 1841924 | tf_op jit(solution)/shard_map/tjk,kcs->tcjs/dot_general | solution.py:64
  111.7 1.0 fusion.11
  112.8 4.0 %fusion.10 = f32[11,5,32,128]{3,2,0,1:T(8,128)S(1)} fusion(f32[11,5,32,128]{3,2,0,1:T(8,128)S(1)} %bitcast.113, f32[5,128,11,32]{1,3,2,0:T(8,128)S(1)} %fusion.11, f32[11,5,32,2]{3,2,0,1:T(8,128)S(1)} %copy-done.3, f32[11,5,32,2]{3,2,0,1:T(8,128)S(1)} %copy.87, f32[11,5,2,128]{3,2,0,1:T(2,128)S(1)} %collective-permute-done.1, ...), kind=kOutput, calls=%fused_computation.17 | convolution fusion | flops 34696640 | bytes 5587204 | tf_op jit(solution)/shard_map/tjk,kcs->tcjs/dot_general | solution.py:64
  116.8 7.7 %copy.115 = f32[11,5,32,128]{0,1,3,2:T(8,128)} copy(f32[11,5,32,128]{3,2,0,1:T(8,128)S(1)} %fusion.10) | data formatting | bytes 1802240 | tf_op jit(solution)/shard_map/reshape | solution.py:129
  124.5 7.5 %gather_fusion = f32[256,11,5]{1,2,0:T(8,128)} fusion(f32[11,5,4096]{0,1,2:T(8,128)} %bitcast.109, s32[1024]{0:T(1024)S(1)} %pad_clamp_fusion.1), kind=kCustom, calls=%fused_computation | custom fusion | bytes 113664 | tf_op jit(solution)/shard_map/jit(_take)/gather | solution.py:132
  132.0 1.6 fusion.102
  133.6 1.2 reshape.402
  134.8 15.8 %all-to-all-start = ((f32[64,1,220]{2,1,0:T(1,128)}), f32[64,1,220]{2,1,0:T(1,128)S(1)}, u32[]{:S(2)}, u32[]{:S(2)}) async-start(f32[64,1,220]{2,1,0:T(1,128)} %reshape.402), calls=%async_computation | async-start | bytes 131072 | tf_op jit(solution)/shard_map/all_to_all | solution.py:133
  150.7 1.0 copy.105
  151.7 12.6 %all-to-all-done = f32[64,1,220]{2,1,0:T(1,128)S(1)} async-done(((f32[64,1,220]{2,1,0:T(1,128)}), f32[64,1,220]{2,1,0:T(1,128)S(1)}, u32[]{:S(2)}, u32[]{:S(2)}) %all-to-all-start) | async-done | bytes 56352 | tf_op jit(solution)/shard_map/all_to_all | solution.py:133
  164.8 0.8 reduce
  165.6 0.7 reshape.403
  166.3 1.0 gather_fusion.1
  167.7 0.7 copy.106
  (58 shorter events, 4.8 us)
Async XLA Ops:
  7.2 53.6 %copy-start = (f32[5,5]{1,0:T(8,128)S(1)}, f32[5,5]{1,0:T(8,128)}, u32[]{:S(2)}) copy-start(f32[5,5]{1,0:T(8,128)} %param.13) | copy-start | bytes 304
  7.2 100.8 %all-reduce.3.cloned.1.call-start = ((), (), s32[]{:S(2)}) async-start(), calls=%async_computation.1 | async-start | bytes 327680 | tf_op jit(solution)/shard_map/psum | solution.py:23
  9.7 38.2 %copy-start.7 = (f32[1,2,5,5,128]{4,1,3,2,0:T(2,128)S(1)}, f32[1,2,5,5,128]{4,1,3,2,0:T(2,128)}, u32[]{:S(2)}) copy-start(f32[1,2,5,5,128]{4,1,3,2,0:T(2,128)} %param.9) | copy-start | bytes 76804
  9.7 40.7 %copy-start.9 = (s32[4]{0:T(128)S(1)}, s32[4]{0:T(128)}, u32[]{:S(2)}) copy-start(s32[4]{0:T(128)} %param.10) | copy-start | bytes 52
  9.7 41.4 %copy-start.8 = (s32[4,5]{1,0:T(4,128)S(1)}, s32[4,5]{1,0:T(4,128)}, u32[]{:S(2)}) copy-start(s32[4,5]{1,0:T(4,128)} %param.11) | copy-start | bytes 244
  9.7 41.4 %copy-start.1 = (f32[1,11,5,32,128]{4,3,2,1,0:T(8,128)S(1)}, f32[1,11,5,32,128]{4,3,2,1,0:T(8,128)}, u32[]{:S(2)}) copy-start(f32[1,11,5,32,128]{4,3,2,1,0:T(8,128)} %param.8) | copy-start | bytes 2703364
  11.4 46.2 %collective-permute-start.2 = (f32[11,5,32,2]{2,3,1,0:T(2,128)S(1)}, f32[11,5,32,2]{2,3,1,0:T(2,128)S(1)}, u32[]{:S(2)}, u32[]{:S(2)}) collective-permute-start(f32[11,5,32,2]{2,3,1,0:T(2,128)S(1)} %copy.86), channel_id=1, source_target_pairs={{1,0},{2,1},{3,2},{5,4},{6,5},{7,6},{9,8},{10,9},{11,10},{13,12},{... | collective-permute-start | bytes 42248 | tf_op jit(solution)/shard_map/ppermute | solution.py:34
  27.8 30.2 %collective-permute-start.3 = (f32[11,5,32,2]{2,3,1,0:T(2,128)S(1)}, f32[11,5,32,2]{2,3,1,0:T(2,128)S(1)}, u32[]{:S(2)}, u32[]{:S(2)}) collective-permute-start(f32[11,5,32,2]{2,3,1,0:T(2,128)S(1)} %copy.88), channel_id=1, source_target_pairs={{0,1},{1,2},{2,3},{4,5},{5,6},{6,7},{8,9},{9,10},{10,11},{12,13},{... | collective-permute-start | bytes 42248 | tf_op jit(solution)/shard_map/ppermute | solution.py:33
  34.2 24.2 %collective-permute-start = (f32[11,5,2,128]{3,2,0,1:T(2,128)S(1)}, f32[11,5,2,128]{3,2,0,1:T(2,128)S(1)}, u32[]{:S(2)}, u32[]{:S(2)}) collective-permute-start(f32[11,5,2,128]{3,2,0,1:T(2,128)S(1)} %get-tuple-element.18), channel_id=1, source_target_pairs={{4,0},{8,4},{12,8},{16,12},{20,16},{24,20},{28,24},{32,28},{36,32}... | collective-permute-start | bytes 168968 | tf_op jit(solution)/shard_map/ppermute | solution.py:34
  45.9 13.6 %collective-permute-start.1 = (f32[11,5,2,128]{3,2,0,1:T(2,128)S(1)}, f32[11,5,2,128]{3,2,0,1:T(2,128)S(1)}, u32[]{:S(2)}, u32[]{:S(2)}) collective-permute-start(f32[11,5,2,128]{3,2,0,1:T(2,128)S(1)} %get-tuple-element.19), channel_id=1, source_target_pairs={{0,4},{4,8},{8,12},{12,16},{16,20},{20,24},{24,28},{28,32},{32,36}... | collective-permute-start | bytes 168968 | tf_op jit(solution)/shard_map/ppermute | solution.py:33
  49.7 4.1 %copy-start.11 = (s32[1,1,1,256]{3,2,1,0:T(1,128)S(1)}, s32[1,1,1,256]{3,2,1,0:T(1,128)}, u32[]{:S(2)}) copy-start(s32[1,1,1,256]{3,2,1,0:T(1,128)} %param.14) | copy-start | bytes 3076
  49.7 4.1 %copy-start.12 = (s32[1,1,1,256]{3,2,1,0:T(1,128)S(1)}, s32[1,1,1,256]{3,2,1,0:T(1,128)}, u32[]{:S(2)}) copy-start(s32[1,1,1,256]{3,2,1,0:T(1,128)} %param.15) | copy-start | bytes 3076
  58.4 2.3 %copy-start.2 = (f32[11,5,32,2]{3,2,0,1:T(8,128)}, f32[11,5,32,2]{3,2,0,1:T(8,128)S(1)}, u32[]{:S(2)}) copy-start(f32[11,5,32,2]{3,2,0,1:T(8,128)S(1)} %copy.89) | copy-start | bytes 42244
  60.7 3.0 %copy-start.10 = (f32[5,5]{1,0:T(8,128)S(1)}, f32[5,5]{1,0:T(8,128)}, u32[]{:S(2)}) copy-start(f32[5,5]{1,0:T(8,128)} %param.12) | copy-start | bytes 304
  108.0 3.7 %copy-start.6 = (f32[10,5,128]{2,0,1:T(8,128)S(1)}, f32[10,5,128]{2,0,1:T(8,128)}, u32[]{:S(2)}) copy-start(f32[10,5,128]{2,0,1:T(8,128)} %get-tuple-element.14) | copy-start | bytes 76804
  109.7 2.9 %copy-start.4 = (f32[11,32,128,5]{2,3,1,0:T(8,128)S(1)}, f32[11,32,128,5]{2,3,1,0:T(8,128)}, u32[]{:S(2)}) copy-start(f32[11,32,128,5]{2,3,1,0:T(8,128)} %fusion) | copy-start | bytes 2703364
  109.7 2.9 %copy-start.5 = (f32[11,32,128,5]{2,3,1,0:T(8,128)S(1)}, f32[11,32,128,5]{2,3,1,0:T(8,128)}, u32[]{:S(2)}) copy-start(f32[11,32,128,5]{2,3,1,0:T(8,128)} %fusion.2) | copy-start | bytes 2703364
  111.6 1.2 copy-start.3
  111.6 1.2 copy-start.13
  134.8 29.5 %all-to-all-start = ((f32[64,1,220]{2,1,0:T(1,128)}), f32[64,1,220]{2,1,0:T(1,128)S(1)}, u32[]{:S(2)}, u32[]{:S(2)}) async-start(f32[64,1,220]{2,1,0:T(1,128)} %reshape.402), calls=%async_computation | async-start | bytes 131072 | tf_op jit(solution)/shard_map/all_to_all | solution.py:133
Sparse Core Ops, SparseCore 0:
  50.5 57.4 all-reduce.2
where the time goes:
time: 178 us; the launch traced here: 175 us
  waiting for transfers between devices  55.1 us (31%)
  starting transfers between devices  51.9 us (29%)
  local copies, waits for them, and re-layouts  29.3 us (16%)
  matrix products  17.2 us (10%)
  between operations  14.4 us (8%)
  other arithmetic  7.22 us (4%)
    psum x1, waiting for transfers between devices, from_root(): return lax.psum(jnp.where(mine, value, jnp.zeros_like(value)), axis)  41.4 us
    ppermute x2, starting transfers between devices, with_halo(): after = lax.ppermute(leading, axis, down)  27.7 us
    all_to_all x1, starting transfers between devices, local(): lax.all_to_all(outgoing, 'pitch', split_axis=2, concat_axis=2, tiled=True)  15.8 us
    all_to_all x1, waiting for transfers between devices, local(): lax.all_to_all(outgoing, 'pitch', split_axis=2, concat_axis=2, tiled=True)  12.6 us
    dot_general x4, matrix products, interface_values(): jnp.einsum('tjk,kcs->tcjs', table, coeffs, precision=lax.Precision.HIGHEST)  8.58 us
    ppermute x2, starting transfers between devices, with_halo(): before = lax.ppermute(last, axis, up)  8.25 us
    reshape x1, local copies, waits for them, and re-layouts, local(): updated_solution.reshape(SNAPSHOT_COUNT, QUANTITY_COUNT, angular_portion...  7.68 us
    gather x1, local copies, waits for them, and re-layouts, local(): outgoing = jnp.take(linear_mesh_points, send_cell[0, 0, 0], axis=2)  7.49 us
  transfers between devices with their start and end apart: 6, of which 3 were waited for; matrix products, arithmetic and copies ran while one was open for 11% of the time, Pallas kernels for 0%

commit v1 on v0

v1 whole, which is shorter than its diff:
```python
import functools
import math

import jax
import jax.numpy as jnp
import numpy as np
from jax import lax
from jax.experimental import pallas as pl
from jax.experimental.pallas import tpu as pltpu
from jax.sharding import PartitionSpec as P

MESH = pl.DeviceIdType.MESH
F32, BF16, I32 = jnp.float32, jnp.bfloat16, jnp.int32

H = 5
NT = 11
NC = 5
NJ = 32
NS = 128
NK = 256
TC = NT * NC
PAD = 64
ROWS = TC * NJ

step_size = 0.25
damping = 1.0 / 16.0
coupling = 0.5
frequency = 0.5
far_weight = 0.5

d_entries = [
    float(np.float32(0.5 * frequency * math.cos(math.pi * n) / math.sin(math.pi * n / NT)))
    for n in range(1, NT // 2 + 1)
]


def iota(shape, dim):
    return lax.broadcasted_iota(I32, shape, dim)


def split(x):
    high = x.astype(BF16)
    return high, (x - high.astype(F32)).astype(BF16)


def dot(a, b):
    return lax.dot_general(a, b, (((1,), (0,)), ((), ())), preferred_element_type=F32)


def one_hot(condition):
    return jnp.where(condition, 1.0, 0.0).astype(BF16)


def section(
    sizes,
    blades,
    harmonics,
    pitch_jac,
    span_jac,
    u_hbm,
    spec_hbm,
    cell_hbm,
    order_hbm,
    out_hbm,
    wall_ref,
    u_ref,
    upd_ref,
    heard_ref,
    specs,
    coeff_ref,
    rhs_ref,
    table_ref,
    cell_ref,
    order_ref,
    cell_s,
    cell_j,
    cell_edge,
    slot_ref,
    mix_p,
    mix_s,
    pitch_out,
    pitch_in,
    span_out,
    span_in,
    edge_ref,
    corr_ref,
    g_part,
    g_ref,
    turn_ref,
    outgoing,
    arrived,
    load_sem,
    pitch_send,
    pitch_recv,
    span_send,
    span_recv,
    row_send,
    row_recv,
    wall_send,
    wall_recv,
    out_sem,
):
    n_row, n_pitch, n_span = sizes
    handoff = NK // n_pitch
    half = handoff // 2
    r, p, s = lax.axis_index("row"), lax.axis_index("pitch"), lax.axis_index("span")

    def pitch_peer(k):
        return (r, lax.rem(p + k, n_pitch), s)

    def row_peer(k):
        return (lax.rem(r + k, n_row), p, s)

    barrier = pltpu.get_barrier_semaphore()
    span_ring = (1, n_span - 1) if n_span > 2 else (1,)
    for k in span_ring:
        pl.semaphore_signal(
            barrier, inc=1, device_id=(r, p, lax.rem(s + k, n_span)), device_id_type=MESH
        )
    for k in range(1, n_row):
        pl.semaphore_signal(barrier, inc=1, device_id=row_peer(k), device_id_type=MESH)

    def greet(k, carry):
        pl.semaphore_signal(barrier, inc=1, device_id=pitch_peer(k), device_id_type=MESH)
        return carry

    lax.fori_loop(1, n_pitch, greet, 0)

    load_u = pltpu.make_async_copy(u_hbm, u_ref, load_sem.at[0])
    load_cell = pltpu.make_async_copy(cell_hbm, cell_ref, load_sem.at[1])
    load_order = pltpu.make_async_copy(order_hbm, order_ref, load_sem.at[2])
    load_u.start()
    load_cell.start()
    load_order.start()

    lane = iota((1, NS), 1)

    pitch_out[...] = jnp.zeros_like(pitch_out)
    edge_ref[...] = jnp.zeros_like(edge_ref)
    g_ref[...] = jnp.zeros_like(g_ref)
    coeff_ref[...] = jnp.zeros_like(coeff_ref)

    @pl.when(s == 0)
    def _():
        span_in[0] = jnp.zeros_like(span_in[0])

    @pl.when(s == n_span - 1)
    def _():
        span_in[1] = jnp.zeros_like(span_in[1])

    load_u.wait()
    for layer in range(2):
        pitch_out[0, layer, 0:TC, :] = u_ref[pl.ds(NJ - 2 + layer, TC, stride=NJ), :]
        pitch_out[1, layer, 0:TC, :] = u_ref[pl.ds(layer, TC, stride=NJ), :]
    edges = jnp.zeros((TC, NS), F32)
    for j in range(NJ):
        turned = pltpu.roll(u_ref[pl.ds(j, TC, stride=NJ), :], (2 + 4 * j) % NS, 1)
        edges = jnp.where((lane >= 4 * j) & (lane < 4 * j + 4), turned, edges)
    edge_ref[0:TC, :] = edges
    e4 = lax.rem(lane, 4)
    low, high = edge_ref[0 : PAD // 2, :], edge_ref[PAD // 2 : PAD, :]
    span_out[0] = jnp.where(e4 < 2, low, pltpu.roll(high, 2, 1))
    span_out[1] = jnp.where(e4 >= 2, low, pltpu.roll(high, NS - 2, 1))

    pl.semaphore_wait(barrier, len(span_ring) + n_row - 1 + n_pitch - 1)
    right = pltpu.make_async_remote_copy(
        span_out.at[0],
        span_in.at[0],
        span_send.at[0],
        span_recv.at[0],
        device_id=(r, p, lax.rem(s + 1, n_span)),
        device_id_type=MESH,
    )
    left = pltpu.make_async_remote_copy(
        span_out.at[1],
        span_in.at[1],
        span_send.at[1],
        span_recv.at[1],
        device_id=(r, p, lax.rem(s + n_span - 1, n_span)),
        device_id_type=MESH,
    )

    @pl.when(s < n_span - 1)
    def _():
        right.start()

    @pl.when(s > 0)
    def _():
        left.start()

    halos = []
    for way, k in ((0, 1), (1, n_pitch - 1)):
        copy = pltpu.make_async_remote_copy(
            pitch_out.at[way],
            pitch_in.at[way],
            pitch_send.at[way],
            pitch_recv.at[way],
            device_id=pitch_peer(k),
            device_id_type=MESH,
        )
        copy.start()
        halos.append(copy)
    spectra = []
    for k in range(1, n_row):
        copy = pltpu.make_async_remote_copy(
            spec_hbm,
            specs.at[r],
            row_send.at[k],
            row_recv,
            device_id=row_peer(k),
            device_id_type=MESH,
        )
        copy.start()
        spectra.append(copy)
    pltpu.make_async_copy(spec_hbm, specs.at[r], row_recv).start()

    load_cell.wait()
    load_order.wait()
    cell = cell_ref[...]
    cj, cs = cell // NS, lax.rem(cell, NS)
    cell_s[...] = one_hot((iota((2 * NS, NK), 0) & (NS - 1)) == cs)
    cell_j[...] = jnp.where(iota((NJ, NK), 0) == cj, 1.0, 0.0)
    place = iota((2 * NS, NK), 0) & (NS - 1)
    e_row = place & 3
    column = jnp.where(e_row < 2, e_row, NS - 4 + e_row)
    cell_edge[...] = one_hot((place // 4 == cj) & (column == cs))
    rho = iota((NK, NK), 0)
    rest = rho & (NS - 1)
    slot = (rest & (n_pitch - 1)) * handoff + (rest // n_pitch) * 2 + rho // NS
    slot_ref[...] = one_hot(slot == order_ref[...])

    mr, mc = iota((PAD, NS), 0), iota((PAD, NS), 1) & (PAD - 1)
    tr, tcol = (mr * 205) >> 10, (mc * 205) >> 10
    cr, cc = mr - 5 * tr, mc - 5 * tcol
    same = (tr == tcol) & (mr < TC) & (mc < TC)
    pair = jnp.where(same, cr * NC + cc, -1)
    for jac, mix in ((pitch_jac, mix_p), (span_jac, mix_s)):
        m = jnp.zeros((PAD, NS), F32)
        for a in range(NC):
            for c in range(NC):
                m = jnp.where(pair == a * NC + c, jac[a, c], m)
        mh, ml = split(m)
        mix[:, 0:NS] = mh
        mix[:, NS : 2 * NS] = ml

    l64 = lane & (PAD - 1)
    lg, lk = l64 // 16, l64 & 15
    order_of = jnp.zeros((1, NS), I32)
    turns_of = jnp.zeros((1, NS), I32)
    weight = jnp.zeros((1, NS), F32)
    for g in range(n_row):
        distance = jnp.abs(r - g)
        w = jnp.where(distance == 1, 1.0, jnp.where(distance >= 2, far_weight, 0.0)).astype(F32)
        weight = jnp.where((lg == g) & (lk < 2 * H), w, weight)
        for n in range(H):
            here = (lg == g) & (lk // 2 == n)
            order_of = jnp.where(here, harmonics[g, n], order_of)
            turns_of = jnp.where(here, harmonics[g, n] * blades[g], turns_of)
    whole = n_pitch * NJ
    cells = p * NJ + iota((NJ, NS), 0)
    phase_j = ((turns_of * cells) & (whole - 1)).astype(F32) * (2.0 * math.pi / whole)
    phase_j = phase_j - (lk & 1).astype(F32) * (0.5 * math.pi)
    times = order_of * iota((16, NS), 0)
    times = times - NT * ((times * 5958) >> 16)
    phase_t = times.astype(F32) * (2.0 * math.pi / NT)
    cos_j, sin_j = weight * jnp.cos(phase_j), weight * jnp.sin(phase_j)
    cos_t, sin_t = jnp.cos(phase_t), jnp.sin(phase_t)
    for t in range(NT):
        high, low = split(cos_t[t : t + 1] * cos_j - sin_t[t : t + 1] * sin_j)
        table_ref[t * NJ : (t + 1) * NJ, 0:NS] = high
        table_ref[t * NJ : (t + 1) * NJ, NS : 2 * NS] = low

    row = iota((1, NJ, 1), 1)

    def at(t):
        return pl.ds(pl.multiple_of(t * (NC * NJ), NC * NJ), NC * NJ)

    def interior(t, carry):
        x = u_ref[at(t), :]
        m1 = jnp.where(lane >= 1, pltpu.roll(x, 1, 1), 0.0)
        m2 = jnp.where(lane >= 2, pltpu.roll(x, 2, 1), 0.0)
        p1 = jnp.where(lane < NS - 1, pltpu.roll(x, NS - 1, 1), 0.0)
        p2 = jnp.where(lane < NS - 2, pltpu.roll(x, NS - 2, 1), 0.0)
        d1s = (0.5 * (p1 - m1)).reshape(NC, NJ, NS)
        fourth = ((p2 + m2) - 4.0 * (p1 + m1)).reshape(NC, NJ, NS)
        x = x.reshape(NC, NJ, NS)
        m1 = jnp.where(row >= 1, pltpu.roll(x, 1, 1), 0.0)
        m2 = jnp.where(row >= 2, pltpu.roll(x, 2, 1), 0.0)
        p1 = jnp.where(row < NJ - 1, pltpu.roll(x, NJ - 1, 1), 0.0)
        p2 = jnp.where(row < NJ - 2, pltpu.roll(x, NJ - 2, 1), 0.0)
        d1p = 0.5 * (p1 - m1)
        fourth = fourth + ((p2 + m2) - 4.0 * (p1 + m1))
        change = damping * fourth + (12.0 * damping + 2.0 * coupling) * x
        for n in range(1, NT // 2 + 1):
            before = u_ref[at(lax.rem(t + NT - n, NT)), :]
            after = u_ref[at(lax.rem(t + n, NT)), :]
            change = change + d_entries[n - 1] * (before - after).reshape(NC, NJ, NS)
        for a in range(NC):
            flux = change[a]
            for c in range(NC):
                flux = flux + pitch_jac[a, c] * d1p[c] + span_jac[a, c] * d1s[c]
            upd_ref[pl.ds(pl.multiple_of((t * NC + a) * NJ, NJ), NJ), :] = x[a] - step_size * flux
        return carry

    lax.fori_loop(0, NT, interior, 0)

    pltpu.make_async_copy(specs, specs, row_recv).wait()
    for g in range(n_row):
        for n in range(H):
            for c in range(NC):
                coeff_ref[16 * g + 2 * n : 16 * g + 2 * n + 2, c * NS : (c + 1) * NS] = specs[
                    g, n * NC + c
                ]
    high, low = split(coeff_ref[...])
    for k in range(2):
        rhs_ref[2 * PAD * k : 2 * PAD * k + PAD, :] = high
        rhs_ref[2 * PAD * k + PAD : 2 * PAD * (k + 1), :] = low
    heard_ref[...] = dot(table_ref[...], rhs_ref[...])

    def gather(t, carry):
        heard = heard_ref[pl.ds(pl.multiple_of(t * NJ, NJ), NJ), :]
        heard = jnp.concatenate([heard[:, c * NS : (c + 1) * NS] for c in range(NC)], axis=0)
        x = upd_ref[at(t), :] + (step_size * coupling) * heard
        upd_ref[at(t), :] = x
        high, low = split(x)
        found = dot(jnp.concatenate([high, low], axis=1), cell_s[...])
        found = found.reshape(NC, NJ, NK) * cell_j[...]
        g_part[t] = jnp.sum(found, axis=1)
        return carry

    lax.fori_loop(0, NT, gather, 0)
    for t in range(NT):
        g_ref[t * NC : (t + 1) * NC, :] = g_part[t]

    @pl.when(s < n_span - 1)
    def _():
        left_in = pltpu.make_async_copy(span_in.at[1], span_in.at[1], span_recv.at[1])
        left_in.wait()

    @pl.when(s > 0)
    def _():
        right_in = pltpu.make_async_copy(span_in.at[0], span_in.at[0], span_recv.at[0])
        right_in.wait()

    from_left, from_right = span_in[0], span_in[1]
    x = jnp.concatenate(
        [
            jnp.where(e4 < 2, from_left, from_right),
            jnp.where(e4 < 2, pltpu.roll(from_left, NS - 2, 1), pltpu.roll(from_right, 2, 1)),
        ],
        axis=0,
    )
    y = jnp.where(e4 == 0, pltpu.roll(x, NS - 1, 1), jnp.where(e4 == 3, pltpu.roll(x, 1, 1), 0.0))
    sign = jnp.where(e4 == 0, -0.5, jnp.where(e4 == 3, 0.5, 0.0))
    high, low = split(y)
    mixed = dot(mix_s[...], jnp.concatenate([high, low, high, low], axis=0))
    corr_ref[4] = -step_size * (sign * mixed + damping * (x - 4.0 * y))

    for copy in halos:
        copy.wait_recv()
    inner = jnp.concatenate([pitch_in[0, 1], pitch_in[1, 0]], axis=1)
    high, low = split(inner)
    mixed = dot(mix_p[...], jnp.concatenate([high, low, high, low], axis=0))
    corr_ref[0] = -step_size * (
        -0.5 * mixed[:, 0:NS] + damping * (pitch_in[0, 0] - 4.0 * pitch_in[0, 1])
    )
    corr_ref[1] = (-step_size * damping) * pitch_in[0, 1]
    corr_ref[2] = (-step_size * damping) * pitch_in[1, 0]
    corr_ref[3] = -step_size * (
        0.5 * mixed[:, NS : 2 * NS] + damping * (pitch_in[1, 1] - 4.0 * pitch_in[1, 0])
    )

    high, low = split(corr_ref[4])
    total = g_ref[...] + dot(jnp.concatenate([high, low], axis=1), cell_edge[...])
    high, low = split(corr_ref[0:4].reshape(4 * PAD, NS))
    found = dot(jnp.concatenate([high, low], axis=1), cell_s[...])
    for e, at_row in enumerate((0, 1, NJ - 2, NJ - 1)):
        total = total + found[e * PAD : (e + 1) * PAD] * cell_j[at_row : at_row + 1, :]

    turn_ref[...] = jnp.concatenate([total, pltpu.roll(total, NK - 1, 1)], axis=0).T
    for i in range(half):
        outgoing[:, i, :] = turn_ref[pl.ds(2 * i, n_pitch, stride=handoff), :]

    def send(k, carry):
        q = lax.rem(p + k, n_pitch)
        pltpu.make_async_remote_copy(
            outgoing.at[q],
            arrived.at[p],
            wall_send,
            wall_recv,
            device_id=(r, q, s),
            device_id_type=MESH,
        ).start()
        return carry

    lax.fori_loop(1, n_pitch, send, 0)
    pltpu.make_async_copy(outgoing.at[p], arrived.at[p], wall_recv).start()

    for e, at_row in enumerate((0, 1, NJ - 2, NJ - 1)):
        rows = pl.ds(at_row, TC, stride=NJ)
        upd_ref[rows, :] = upd_ref[rows, :] + corr_ref[e, 0:TC, :]
    e_lane = iota((2 * NS, NS), 0) & 3
    to_column = one_hot(iota((2 * NS, NS), 1) == jnp.where(e_lane < 2, e_lane, NS - 4 + e_lane))
    own = lane // 4 == iota((NJ, NS), 0)
    for t in range(NT):
        spread = jnp.concatenate(
            [
                jnp.where(own, corr_ref[4, t * NC + c : t * NC + c + 1, :], 0.0)
                for c in range(NC)
            ],
            axis=0,
        )
        high, low = split(spread)
        rows = slice(t * NC * NJ, (t + 1) * NC * NJ)
        upd_ref[rows, :] = upd_ref[rows, :] + dot(
            jnp.concatenate([high, low], axis=1), to_column
        )
    store = pltpu.make_async_copy(upd_ref, out_hbm, out_sem)
    store.start()

    pltpu.make_async_copy(arrived, arrived, wall_recv).wait()
    slots = jnp.concatenate([arrived[:, i, :] for i in range(half)], axis=0).T
    high, low = split(jnp.concatenate([slots[0:PAD], slots[PAD : 2 * PAD]], axis=1))
    placed = dot(jnp.concatenate([high, low], axis=0), slot_ref[...])
    placed = placed[0:PAD] + placed[PAD : 2 * PAD]
    for k in range(NK // NS):
        wall_ref[:, k, :] = placed[0:TC, k * NS : (k + 1) * NS]

    some = outgoing.at[pl.ds(0, n_pitch - 1)]
    pltpu.make_async_copy(some, some, wall_send).wait()
    for copy in halos + spectra:
        copy.wait_send()

    @pl.when(s < n_span - 1)
    def _():
        right.wait_send()

    @pl.when(s > 0)
    def _():
        left.wait_send()

    store.wait()


def local(sizes, unknowns, spectrum, blades, harmonics, pitch_jac, span_jac, send_cell, recv_order):
    n_row, n_pitch, n_span = sizes
    half = NK // n_pitch // 2
    vmem, dma = pltpu.VMEM, pltpu.SemaphoreType.DMA
    anywhere = pl.BlockSpec(memory_space=pl.ANY)
    scalars = pl.BlockSpec(memory_space=pltpu.SMEM)
    updated, wall = pl.pallas_call(
        functools.partial(section, sizes),
        out_shape=(
            jax.ShapeDtypeStruct((ROWS, NS), F32),
            jax.ShapeDtypeStruct((TC, NK // NS, NS), F32),
        ),
        in_specs=[scalars] * 4 + [anywhere] * 4,
        out_specs=(anywhere, pl.BlockSpec(memory_space=pltpu.VMEM)),
        scratch_shapes=[
            vmem((ROWS, NS), F32),
            vmem((ROWS, NS), F32),
            vmem((NT * NJ, NC * NS), F32),
            vmem((n_row, H * NC, 2, NS), F32),
            vmem((PAD, NC * NS), F32),
            vmem((4 * PAD, NC * NS), BF16),
            vmem((NT * NJ, 2 * NS), BF16),
            vmem((1, NK), I32),
            vmem((1, NK), I32),
            vmem((2 * NS, NK), BF16),
            vmem((NJ, NK), F32),
            vmem((2 * NS, NK), BF16),
            vmem((NK, NK), BF16),
            vmem((PAD, 2 * NS), BF16),
            vmem((PAD, 2 * NS), BF16),
            vmem((2, 2, PAD, NS), F32),
            vmem((2, 2, PAD, NS), F32),
            vmem((2, PAD // 2, NS), F32),
            vmem((2, PAD // 2, NS), F32),
            vmem((PAD, NS), F32),
            vmem((5, PAD, NS), F32),
            vmem((NT, NC, NK), F32),
            vmem((PAD, NK), F32),
            vmem((NK, NS), F32),
            vmem((n_pitch, half, NS), F32),
            vmem((n_pitch, half, NS), F32),
            dma((3,)),
            dma((2,)),
            dma((2,)),
            dma((2,)),
            dma((2,)),
            dma((n_row,)),
            dma,
            dma,
            dma,
            dma,
        ],
        compiler_params=pltpu.CompilerParams(
            collective_id=1, has_side_effects=True, vmem_limit_bytes=32 * 1024 * 1024
        ),
        name="flux_section",
    )(
        blades,
        harmonics,
        pitch_jac,
        span_jac,
        unknowns.reshape(ROWS, NS),
        jnp.transpose(spectrum[0], (1, 2, 0, 3)).reshape(H * NC, 2, NS),
        send_cell.reshape(1, NK),
        recv_order.reshape(1, NK),
    )
    return (
        updated.reshape(unknowns.shape),
        wall.reshape(1, 1, NT, NC, NK),
    )


def solution(mesh):
    sizes = (mesh.shape["row"], mesh.shape["pitch"], mesh.shape["span"])
    return jax.shard_map(
        functools.partial(local, sizes),
        mesh=mesh,
        in_specs=(
            P("row", None, None, "pitch", "span"),
            P("row", None, None, None, "span"),
            P(),
            P(),
            P(),
            P(),
            P("row", "span", "pitch", None),
            P("row", "span", "pitch", None),
        ),
        out_specs=(P("row", None, None, "pitch", "span"), P("row", "span", None, None, "pitch")),
        check_vma=False,
    )
```

time: 178 us -> 48.5 us (0.27); the launches traced: 175 us -> 48.2 us
  waiting for transfers between devices: 55.1 us -> 0 us
  starting transfers between devices: 51.9 us -> 0 us
  Pallas kernels: 0 us -> 42 us
  local copies, waits for them, and re-layouts: 29.3 us -> 5.5 us
  matrix products: 17.2 us -> 0 us
  between operations: 14.4 us -> 0.68 us
  other arithmetic: 7.22 us -> 0 us
    pallas_call x0 -> x1, Pallas kernels: none -> 42 us  [local(): pl.pallas_call(functools.partial(section, sizes), out_shape=(jax.ShapeDty...]
    psum x1 -> x0, waiting for transfers between devices: 41.4 us -> none  [from_root(): return lax.psum(jnp.where(mine, value, jnp.zeros_like(value)), axis)]
    ppermute x4 -> x0, starting transfers between devices: 36 us -> none  [the longest x2 27.7 us: with_halo(): after = lax.ppermute(leading, axis, down)]
    dot_general x7 -> x0, matrix products: 17.2 us -> none  [the longest x4 8.58 us: interface_values(): jnp.einsum('tjk,kcs->tcjs', table, coeffs, precision=lax.Precision.HIGHEST)]
    all_to_all x1 -> x0, starting transfers between devices: 15.8 us -> none  [local(): lax.all_to_all(outgoing, 'pitch', split_axis=2, concat_axis=2, tiled=True)]
    all_to_all x1 -> x0, waiting for transfers between devices: 12.6 us -> none  [local(): lax.all_to_all(outgoing, 'pitch', split_axis=2, concat_axis=2, tiled=True)]
    reshape x5 -> x0, local copies, waits for them, and re-layouts: 10.2 us -> none  [the longest x1 7.68 us: local(): updated_solution.reshape(SNAPSHOT_COUNT, QUANTITY_COUNT, angular_portion...]
    gather x3 -> x0, local copies, waits for them, and re-layouts: 8.81 us -> none  [the longest x1 7.49 us: local(): outgoing = jnp.take(linear_mesh_points, send_cell[0, 0, 0], axis=2)]
  transfers between devices with their start and end apart: 6 -> 0, of which waited for: 3 -> 0; matrix products, arithmetic and copies ran while one was open for 11% -> 0% of each run, Pallas kernels for 0% -> 0%
where the time goes in v1:
time: 48.5 us; the launch traced here: 48.2 us
  Pallas kernels  42 us (87%)
  local copies, waits for them, and re-layouts  5.5 us (11%)
  between operations  0.68 us (1%)
    pallas_call x1, Pallas kernels, local(): pl.pallas_call(functools.partial(section, sizes), out_shape=(jax.ShapeDty...  42 us
    unnamed x18, local copies, waits for them, and re-layouts  5.5 us

profile of v1, /device:TPU:1, one launch (start us, length us, event | category | flops | bytes accessed | tf_op | source)
XLA Modules:
  0.0 48.2 jit_solution(16471975466667109822)
XLA Ops:
  0.6 0.0 copy-start.2
  0.6 0.0 copy-start.4
  0.7 0.0 copy-start.5
  0.7 0.0 copy-start.7
  0.7 0.6 %copy-done.2 = f32[5,5]{1,0:T(8,128)S(1)} copy-done((f32[5,5]{1,0:T(8,128)S(1)}, f32[5,5]{1,0:T(8,128)}, u32[]{:S(2)}) %copy-start.2) | copy-done | bytes 124
  1.3 0.0 copy-done.4
  1.3 0.0 copy-done.5
  1.3 0.0 copy-done.7
  1.3 0.0 copy-start
  1.3 1.2 %copy-done = f32[1,11,5,32,128]{4,3,2,1,0:T(8,128)S(1)} copy-done((f32[1,11,5,32,128]{4,3,2,1,0:T(8,128)S(1)}, f32[1,11,5,32,128]{4,3,2,1,0:T(8,128)}, u32[]{:S(2)}) %copy-start) | copy-done | bytes 901144
  2.5 0.0 copy-start.1
  2.5 0.7 %copy-done.1 = f32[1,2,5,5,128]{4,1,3,2,0:T(2,128)S(1)} copy-done((f32[1,2,5,5,128]{4,1,3,2,0:T(2,128)S(1)}, f32[1,2,5,5,128]{4,1,3,2,0:T(2,128)}, u32[]{:S(2)}) %copy-start.1) | copy-done | bytes 25624
  3.3 0.0 copy-start.3
  3.3 0.7 %copy-done.3 = f32[5,5]{1,0:T(8,128)S(1)} copy-done((f32[5,5]{1,0:T(8,128)S(1)}, f32[5,5]{1,0:T(8,128)}, u32[]{:S(2)}) %copy-start.3) | copy-done | bytes 124
  3.9 0.0 copy-start.6
  4.0 0.7 %copy-done.6 = s32[1,1,1,256]{3,2,1,0:T(1,128)S(1)} copy-done((s32[1,1,1,256]{3,2,1,0:T(1,128)S(1)}, s32[1,1,1,256]{3,2,1,0:T(1,128)}, u32[]{:S(2)}) %copy-start.6) | copy-done | bytes 1048
  4.6 42.0 %flux_section.1 = (f32[1760,128]{1,0:T(8,128)S(1)}, f32[55,2,128]{2,1,0:T(2,128)S(1)}) custom-call(s32[4]{0:T(128)S(1)} %copy-done.7, s32[4,5]{1,0:T(4,128)S(1)} %copy-done.4, f32[5,5]{1,0:T(8,128)S(1)} %copy-done.2, f32[5,5]{1,0:T(8,128)S(1)} %copy-done.3, f32[1760,128]{1,0:T(8,128)S(1)} %bitcast.11, f32[25,2,128]{2,1,0:T(2,128)S(1)} %bitcast.13, ...), custom_call_target="tpu_custom_call" | custom-call | tf_op jit(solution)/shard_map/flux_section/pallas_call | solution.py:451
  46.7 0.9 %copy.14 = f32[1,11,5,32,128]{4,3,2,1,0:T(8,128)} copy(f32[1,11,5,32,128]{4,3,2,1,0:T(8,128)S(1)} %bitcast.10) | data formatting | bytes 1802240
  47.6 0.6 %copy.15 = f32[1,1,11,5,256]{4,1,3,2,0:T(1,128)} copy(f32[1,1,11,5,256]{4,1,3,2,0:T(1,128)S(1)} %bitcast.12) | data formatting | bytes 112640
Async XLA Ops:
  0.6 0.7 %copy-start.2 = (f32[5,5]{1,0:T(8,128)S(1)}, f32[5,5]{1,0:T(8,128)}, u32[]{:S(2)}) copy-start(f32[5,5]{1,0:T(8,128)} %pitch_jac.1) | copy-start | bytes 304
  0.6 0.7 %copy-start.4 = (s32[4,5]{1,0:T(4,128)S(1)}, s32[4,5]{1,0:T(4,128)}, u32[]{:S(2)}) copy-start(s32[4,5]{1,0:T(4,128)} %harmonics.1) | copy-start | bytes 244
  0.7 0.7 %copy-start.5 = (s32[1,1,1,256]{3,2,1,0:T(1,128)S(1)}, s32[1,1,1,256]{3,2,1,0:T(1,128)}, u32[]{:S(2)}) copy-start(s32[1,1,1,256]{3,2,1,0:T(1,128)} %param.14) | copy-start | bytes 3076
  0.7 0.7 %copy-start.7 = (s32[4]{0:T(128)S(1)}, s32[4]{0:T(128)}, u32[]{:S(2)}) copy-start(s32[4]{0:T(128)} %blades.1) | copy-start | bytes 52
  1.3 1.2 %copy-start = (f32[1,11,5,32,128]{4,3,2,1,0:T(8,128)S(1)}, f32[1,11,5,32,128]{4,3,2,1,0:T(8,128)}, u32[]{:S(2)}) copy-start(f32[1,11,5,32,128]{4,3,2,1,0:T(8,128)} %param.8) | copy-start | bytes 2703364
  2.5 0.7 %copy-start.1 = (f32[1,2,5,5,128]{4,1,3,2,0:T(2,128)S(1)}, f32[1,2,5,5,128]{4,1,3,2,0:T(2,128)}, u32[]{:S(2)}) copy-start(f32[1,2,5,5,128]{4,1,3,2,0:T(2,128)} %param.9) | copy-start | bytes 76804
  3.3 0.7 %copy-start.3 = (f32[5,5]{1,0:T(8,128)S(1)}, f32[5,5]{1,0:T(8,128)}, u32[]{:S(2)}) copy-start(f32[5,5]{1,0:T(8,128)} %span_jac.1) | copy-start | bytes 304
  3.9 0.7 %copy-start.6 = (s32[1,1,1,256]{3,2,1,0:T(1,128)S(1)}, s32[1,1,1,256]{3,2,1,0:T(1,128)}, u32[]{:S(2)}) copy-start(s32[1,1,1,256]{3,2,1,0:T(1,128)} %param.15) | copy-start | bytes 3076

commit v2 on v1

--- a/solution.py
+++ b/solution.py
@@ -21,6 +21,7 @@
 TC = NT * NC
 PAD = 64
 ROWS = TC * NJ
+PARTS = 5
 
 step_size = 0.25
 damping = 1.0 / 16.0
@@ -53,29 +54,29 @@
 
 def section(
     sizes,
+    blades_hbm,
+    harmonics_hbm,
+    pitch_jac_hbm,
+    span_jac_hbm,
+    u_hbm,
+    spec_hbm,
+    cell_hbm,
+    upd_ref,
+    arrived,
     blades,
     harmonics,
     pitch_jac,
     span_jac,
-    u_hbm,
-    spec_hbm,
-    cell_hbm,
-    order_hbm,
-    out_hbm,
-    wall_ref,
     u_ref,
-    upd_ref,
     heard_ref,
     specs,
     coeff_ref,
     rhs_ref,
     table_ref,
     cell_ref,
-    order_ref,
     cell_s,
     cell_j,
     cell_edge,
-    slot_ref,
     mix_p,
     mix_s,
     pitch_out,
@@ -88,7 +89,6 @@
     g_ref,
     turn_ref,
     outgoing,
-    arrived,
     load_sem,
     pitch_send,
     pitch_recv,
@@ -98,7 +98,6 @@
     row_recv,
     wall_send,
     wall_recv,
-    out_sem,
 ):
     n_row, n_pitch, n_span = sizes
     handoff = NK // n_pitch
@@ -117,6 +116,8 @@
         pl.semaphore_signal(
             barrier, inc=1, device_id=(r, p, lax.rem(s + k, n_span)), device_id_type=MESH
         )
+    for k in (1, n_pitch - 1):
+        pl.semaphore_signal(barrier, inc=1, device_id=pitch_peer(k), device_id_type=MESH)
     for k in range(1, n_row):
         pl.semaphore_signal(barrier, inc=1, device_id=row_peer(k), device_id_type=MESH)
 
@@ -124,14 +125,24 @@
         pl.semaphore_signal(barrier, inc=1, device_id=pitch_peer(k), device_id_type=MESH)
         return carry
 
-    lax.fori_loop(1, n_pitch, greet, 0)
+    lax.fori_loop(2, n_pitch - 1, greet, 0)
 
     load_u = pltpu.make_async_copy(u_hbm, u_ref, load_sem.at[0])
     load_cell = pltpu.make_async_copy(cell_hbm, cell_ref, load_sem.at[1])
-    load_order = pltpu.make_async_copy(order_hbm, order_ref, load_sem.at[2])
     load_u.start()
     load_cell.start()
-    load_order.start()
+    scalars = []
+    for i, (src, dst) in enumerate(
+        (
+            (blades_hbm, blades),
+            (harmonics_hbm, harmonics),
+            (pitch_jac_hbm, pitch_jac),
+            (span_jac_hbm, span_jac),
+        )
+    ):
+        copy = pltpu.make_async_copy(src, dst, load_sem.at[2 + i])
+        copy.start()
+        scalars.append(copy)
 
     lane = iota((1, NS), 1)
 
@@ -215,7 +226,8 @@
     pltpu.make_async_copy(spec_hbm, specs.at[r], row_recv).start()
 
     load_cell.wait()
-    load_order.wait()
+    for copy in scalars:
+        copy.wait()
     cell = cell_ref[...]
     cj, cs = cell // NS, lax.rem(cell, NS)
     cell_s[...] = one_hot((iota((2 * NS, NK), 0) & (NS - 1)) == cs)
@@ -224,10 +236,6 @@
     e_row = place & 3
     column = jnp.where(e_row < 2, e_row, NS - 4 + e_row)
     cell_edge[...] = one_hot((place // 4 == cj) & (column == cs))
-    rho = iota((NK, NK), 0)
-    rest = rho & (NS - 1)
-    slot = (rest & (n_pitch - 1)) * handoff + (rest // n_pitch) * 2 + rho // NS
-    slot_ref[...] = one_hot(slot == order_ref[...])
 
     mr, mc = iota((PAD, NS), 0), iota((PAD, NS), 1) & (PAD - 1)
     tr, tcol = (mr * 205) >> 10, (mc * 205) >> 10
@@ -415,17 +423,8 @@
         upd_ref[rows, :] = upd_ref[rows, :] + dot(
             jnp.concatenate([high, low], axis=1), to_column
         )
-    store = pltpu.make_async_copy(upd_ref, out_hbm, out_sem)
-    store.start()
 
     pltpu.make_async_copy(arrived, arrived, wall_recv).wait()
-    slots = jnp.concatenate([arrived[:, i, :] for i in range(half)], axis=0).T
-    high, low = split(jnp.concatenate([slots[0:PAD], slots[PAD : 2 * PAD]], axis=1))
-    placed = dot(jnp.concatenate([high, low], axis=0), slot_ref[...])
-    placed = placed[0:PAD] + placed[PAD : 2 * PAD]
-    for k in range(NK // NS):
-        wall_ref[:, k, :] = placed[0:TC, k * NS : (k + 1) * NS]
-
     some = outgoing.at[pl.ds(0, n_pitch - 1)]
     pltpu.make_async_copy(some, some, wall_send).wait()
     for copy in halos + spectra:
@@ -439,25 +438,50 @@
     def _():
         left.wait_send()
 
-    store.wait()
+
+def finish(sizes, upd_ref, arrived, order_hbm, out_hbm, wall_ref, order_ref, sem):
+    n_pitch = sizes[1]
+    handoff = NK // n_pitch
+    load = pltpu.make_async_copy(order_hbm, order_ref, sem.at[0])
+    load.start()
+    stores = []
+    for i in range(PARTS):
+        part = pl.ds(i * (ROWS // PARTS), ROWS // PARTS)
+        copy = pltpu.make_async_copy(upd_ref.at[part], out_hbm.at[part], sem.at[1 + i])
+        copy.start()
+        stores.append(copy)
+    load.wait()
+
+    slots = jnp.concatenate([arrived[:, i, :] for i in range(handoff // 2)], axis=0).T
+    high, low = split(jnp.concatenate([slots[0:PAD], slots[PAD : 2 * PAD]], axis=1))
+    rho = iota((NK, NK), 0)
+    rest = rho & (NS - 1)
+    slot = (rest & (n_pitch - 1)) * handoff + (rest // n_pitch) * 2 + rho // NS
+    placed = dot(jnp.concatenate([high, low], axis=0), one_hot(slot == order_ref[...]))
+    placed = placed[0:PAD] + placed[PAD : 2 * PAD]
+    for k in range(NK // NS):
+        wall_ref[:, k, :] = placed[0:TC, k * NS : (k + 1) * NS]
+    for copy in stores:
+        copy.wait()
 
 
 def local(sizes, unknowns, spectrum, blades, harmonics, pitch_jac, span_jac, send_cell, recv_order):
     n_row, n_pitch, n_span = sizes
     half = NK // n_pitch // 2
     vmem, dma = pltpu.VMEM, pltpu.SemaphoreType.DMA
-    anywhere = pl.BlockSpec(memory_space=pl.ANY)
-    scalars = pl.BlockSpec(memory_space=pltpu.SMEM)
-    updated, wall = pl.pallas_call(
+    in_hbm = pl.BlockSpec(memory_space=pltpu.HBM)
+    in_vmem = pl.BlockSpec(memory_space=pltpu.VMEM)
+    smem = pltpu.SMEM
+    updated, arrived = pl.pallas_call(
         functools.partial(section, sizes),
-        out_shape=(
-            jax.ShapeDtypeStruct((ROWS, NS), F32),
-            jax.ShapeDtypeStruct((TC, NK // NS, NS), F32),
-        ),
-        in_specs=[scalars] * 4 + [anywhere] * 4,
-        out_specs=(anywhere, pl.BlockSpec(memory_space=pltpu.VMEM)),
+        out_shape=(vmem((ROWS, NS), F32), vmem((n_pitch, half, NS), F32)),
+        in_specs=[in_hbm] * 7,
+        out_specs=(in_vmem, in_vmem),
         scratch_shapes=[
-            vmem((ROWS, NS), F32),
+            smem((n_row,), I32),
+            smem((n_row, H), I32),
+            smem((NC, NC), F32),
+            smem((NC, NC), F32),
             vmem((ROWS, NS), F32),
             vmem((NT * NJ, NC * NS), F32),
             vmem((n_row, H * NC, 2, NS), F32),
@@ -465,11 +489,9 @@
             vmem((4 * PAD, NC * NS), BF16),
             vmem((NT * NJ, 2 * NS), BF16),
             vmem((1, NK), I32),
-            vmem((1, NK), I32),
             vmem((2 * NS, NK), BF16),
             vmem((NJ, NK), F32),
             vmem((2 * NS, NK), BF16),
-            vmem((NK, NK), BF16),
             vmem((PAD, 2 * NS), BF16),
             vmem((PAD, 2 * NS), BF16),
             vmem((2, 2, PAD, NS), F32),
@@ -482,14 +504,12 @@
             vmem((PAD, NK), F32),
             vmem((NK, NS), F32),
             vmem((n_pitch, half, NS), F32),
-            vmem((n_pitch, half, NS), F32),
-            dma((3,)),
+            dma((6,)),
             dma((2,)),
             dma((2,)),
             dma((2,)),
             dma((2,)),
             dma((n_row,)),
-            dma,
             dma,
             dma,
             dma,
@@ -499,14 +519,37 @@
         ),
         name="flux_section",
     )(
-        blades,
-        harmonics,
-        pitch_jac,
-        span_jac,
-        unknowns.reshape(ROWS, NS),
-        jnp.transpose(spectrum[0], (1, 2, 0, 3)).reshape(H * NC, 2, NS),
-        send_cell.reshape(1, NK),
-        recv_order.reshape(1, NK),
+        *(
+            pltpu.with_memory_space_constraint(x, pltpu.HBM)
+            for x in (
+                blades,
+                harmonics,
+                pitch_jac,
+                span_jac,
+                unknowns.reshape(ROWS, NS),
+                jnp.transpose(spectrum[0], (1, 2, 0, 3)).reshape(H * NC, 2, NS),
+                send_cell.reshape(1, NK),
+            )
+        )
+    )
+    updated, wall = pl.pallas_call(
+        functools.partial(finish, sizes),
+        out_shape=(
+            jax.ShapeDtypeStruct((ROWS, NS), F32),
+            jax.ShapeDtypeStruct((TC, NK // NS, NS), F32),
+        ),
+        in_specs=[in_vmem, in_vmem, in_hbm],
+        out_specs=(in_hbm, in_vmem),
+        scratch_shapes=[
+            vmem((1, NK), I32),
+            dma((1 + PARTS,)),
+        ],
+        compiler_params=pltpu.CompilerParams(vmem_limit_bytes=8 * 1024 * 1024),
+        name="wall_order",
+    )(
+        updated,
+        arrived,
+        pltpu.with_memory_space_constraint(recv_order.reshape(1, NK), pltpu.HBM),
     )
     return (
         updated.reshape(unknowns.shape),

time: 48.5 us -> 43.6 us (0.90)
  local copies, waits for them, and re-layouts: 5.5 us -> 0 us
  Pallas kernels: 42 us -> 42.8 us
    unnamed x18 -> x0, local copies, waits for them, and re-layouts: 5.5 us -> none
    pallas_call x1 -> x2, Pallas kernels: 42 us -> 42.8 us  [the longest x1 41.2 us: local(): pl.pallas_call(functools.partial(section, sizes), out_shape=(vmem((ROWS,...]
where the time goes in v2:
time: 43.6 us; the launch traced here: 43.5 us
  Pallas kernels  42.8 us (98%)
  between operations  0.64 us (1%)
    pallas_call x1, Pallas kernels, local(): pl.pallas_call(functools.partial(section, sizes), out_shape=(vmem((ROWS,...  41.2 us
    pallas_call x1, Pallas kernels, local(): pl.pallas_call(functools.partial(finish, sizes), out_shape=(jax.ShapeDtyp...  1.62 us

profile of v2, /device:TPU:1, one launch (start us, length us, event | category | flops | bytes accessed | tf_op | source)
XLA Modules:
  0.0 43.5 jit_solution(1023995192555828)
XLA Ops:
  0.6 41.2 %flux_section.1 = (f32[1760,128]{1,0:T(8,128)S(1)}, f32[64,2,128]{2,1,0:T(2,128)S(1)}) custom-call(s32[4]{0:T(128)} %blades_hbm.1, s32[4,5]{1,0:T(4,128)} %harmonics_hbm.1, f32[5,5]{1,0:T(8,128)} %pitch_jac_hbm.1, f32[5,5]{1,0:T(8,128)} %span_jac_hbm.1, f32[1760,128]{1,0:T(8,128)} %bitcast.10, f32[25,2,128]{2,1,0:T(2,128)} %bitcast.11, s32[1,256]{1,0:T(1,128)} %bitcast.12), custom_call_target="tpu_custom_call" | custom-call | tf_op jit(solution)/shard_map/flux_section/pallas_call | solution.py:475
  41.8 1.6 %wall_order.1 = (f32[1760,128]{1,0:T(8,128)}, f32[55,2,128]{2,1,0:T(2,128)}) custom-call(f32[1760,128]{1,0:T(8,128)S(1)} %get-tuple-element.6.upd_ref, f32[64,2,128]{2,1,0:T(2,128)S(1)} %get-tuple-element.7.arrived, s32[1,256]{1,0:T(1,128)} %bitcast.13), custom_call_target="tpu_custom_call" | custom-call | tf_op jit(solution)/shard_map/wall_order/pallas_call | solution.py:535

commit v3 on v2

--- a/solution.py
+++ b/solution.py
@@ -61,8 +61,10 @@
     u_hbm,
     spec_hbm,
     cell_hbm,
+    order_hbm,
     upd_ref,
     arrived,
+    slot_ref,
     blades,
     harmonics,
     pitch_jac,
@@ -74,6 +76,7 @@
     rhs_ref,
     table_ref,
     cell_ref,
+    order_ref,
     cell_s,
     cell_j,
     cell_edge,
@@ -98,6 +101,7 @@
     row_recv,
     wall_send,
     wall_recv,
+    answer,
 ):
     n_row, n_pitch, n_span = sizes
     handoff = NK // n_pitch
@@ -110,12 +114,27 @@
     def row_peer(k):
         return (lax.rem(r + k, n_row), p, s)
 
+    loads = []
+    for i in range(PARTS):
+        part = pl.ds(i * (ROWS // PARTS), ROWS // PARTS)
+        copy = pltpu.make_async_copy(u_hbm.at[part], u_ref.at[part], load_sem.at[i])
+        copy.start()
+        loads.append(copy)
+
+    middle = n_span // 2
+    mate = s + 1 - 2 * lax.rem(s, 2)
+    below, above = s == middle - 1, s == middle
+
+    def span_peer(k):
+        return (r, p, lax.rem(s + k + n_span, n_span))
+
     barrier = pltpu.get_barrier_semaphore()
-    span_ring = (1, n_span - 1) if n_span > 2 else (1,)
-    for k in span_ring:
-        pl.semaphore_signal(
-            barrier, inc=1, device_id=(r, p, lax.rem(s + k, n_span)), device_id_type=MESH
-        )
+    pl.semaphore_signal(barrier, inc=1, device_id=(r, p, mate), device_id_type=MESH)
+
+    @pl.when(below)
+    def _():
+        pl.semaphore_signal(barrier, inc=1, device_id=span_peer(1), device_id_type=MESH)
+
     for k in (1, n_pitch - 1):
         pl.semaphore_signal(barrier, inc=1, device_id=pitch_peer(k), device_id_type=MESH)
     for k in range(1, n_row):
@@ -127,10 +146,6 @@
 
     lax.fori_loop(2, n_pitch - 1, greet, 0)
 
-    load_u = pltpu.make_async_copy(u_hbm, u_ref, load_sem.at[0])
-    load_cell = pltpu.make_async_copy(cell_hbm, cell_ref, load_sem.at[1])
-    load_u.start()
-    load_cell.start()
     scalars = []
     for i, (src, dst) in enumerate(
         (
@@ -138,48 +153,42 @@
             (harmonics_hbm, harmonics),
             (pitch_jac_hbm, pitch_jac),
             (span_jac_hbm, span_jac),
+            (cell_hbm, cell_ref),
+            (order_hbm, order_ref),
         )
     ):
-        copy = pltpu.make_async_copy(src, dst, load_sem.at[2 + i])
+        copy = pltpu.make_async_copy(src, dst, load_sem.at[PARTS + i])
         copy.start()
         scalars.append(copy)
 
     lane = iota((1, NS), 1)
 
-    pitch_out[...] = jnp.zeros_like(pitch_out)
-    edge_ref[...] = jnp.zeros_like(edge_ref)
-    g_ref[...] = jnp.zeros_like(g_ref)
-    coeff_ref[...] = jnp.zeros_like(coeff_ref)
-
-    @pl.when(s == 0)
-    def _():
-        span_in[0] = jnp.zeros_like(span_in[0])
-
-    @pl.when(s == n_span - 1)
-    def _():
-        span_in[1] = jnp.zeros_like(span_in[1])
-
-    load_u.wait()
-    for layer in range(2):
-        pitch_out[0, layer, 0:TC, :] = u_ref[pl.ds(NJ - 2 + layer, TC, stride=NJ), :]
-        pitch_out[1, layer, 0:TC, :] = u_ref[pl.ds(layer, TC, stride=NJ), :]
+    for copy in loads:
+        copy.wait()
     edges = jnp.zeros((TC, NS), F32)
     for j in range(NJ):
         turned = pltpu.roll(u_ref[pl.ds(j, TC, stride=NJ), :], (2 + 4 * j) % NS, 1)
         edges = jnp.where((lane >= 4 * j) & (lane < 4 * j + 4), turned, edges)
     edge_ref[0:TC, :] = edges
+    edge_ref[TC:PAD, :] = jnp.zeros((PAD - TC, NS), F32)
     e4 = lax.rem(lane, 4)
     low, high = edge_ref[0 : PAD // 2, :], edge_ref[PAD // 2 : PAD, :]
     span_out[0] = jnp.where(e4 < 2, low, pltpu.roll(high, 2, 1))
     span_out[1] = jnp.where(e4 >= 2, low, pltpu.roll(high, NS - 2, 1))
 
-    pl.semaphore_wait(barrier, len(span_ring) + n_row - 1 + n_pitch - 1)
+    greeters = 1 + n_row - 1 + n_pitch - 1
+    pl.semaphore_wait(barrier, jnp.where(above, greeters + 1, greeters))
+
+    @pl.when(above)
+    def _():
+        pl.semaphore_signal(answer, inc=1, device_id=span_peer(-1), device_id_type=MESH)
+
     right = pltpu.make_async_remote_copy(
         span_out.at[0],
         span_in.at[0],
         span_send.at[0],
         span_recv.at[0],
-        device_id=(r, p, lax.rem(s + 1, n_span)),
+        device_id=span_peer(1),
         device_id_type=MESH,
     )
     left = pltpu.make_async_remote_copy(
@@ -187,17 +196,22 @@
         span_in.at[1],
         span_send.at[1],
         span_recv.at[1],
-        device_id=(r, p, lax.rem(s + n_span - 1, n_span)),
+        device_id=span_peer(-1),
         device_id_type=MESH,
     )
 
-    @pl.when(s < n_span - 1)
+    @pl.when(s > 0)
+    def _():
+        left.start()
+
+    @pl.when((s < n_span - 1) & (s != middle - 1))
     def _():
         right.start()
 
-    @pl.when(s > 0)
-    def _():
-        left.start()
+    pitch_out[:, :, TC:PAD, :] = jnp.zeros((2, 2, PAD - TC, NS), F32)
+    for layer in range(2):
+        pitch_out[0, layer, 0:TC, :] = u_ref[pl.ds(NJ - 2 + layer, TC, stride=NJ), :]
+        pitch_out[1, layer, 0:TC, :] = u_ref[pl.ds(layer, TC, stride=NJ), :]
 
     halos = []
     for way, k in ((0, 1), (1, n_pitch - 1)):
@@ -225,7 +239,17 @@
         spectra.append(copy)
     pltpu.make_async_copy(spec_hbm, specs.at[r], row_recv).start()
 
-    load_cell.wait()
+    g_ref[TC:PAD, :] = jnp.zeros((PAD - TC, NK), F32)
+    coeff_ref[...] = jnp.zeros_like(coeff_ref)
+
+    @pl.when(s == 0)
+    def _():
+        span_in[0] = jnp.zeros_like(span_in[0])
+
+    @pl.when(s == n_span - 1)
+    def _():
+        span_in[1] = jnp.zeros_like(span_in[1])
+
     for copy in scalars:
         copy.wait()
     cell = cell_ref[...]
@@ -236,6 +260,10 @@
     e_row = place & 3
     column = jnp.where(e_row < 2, e_row, NS - 4 + e_row)
     cell_edge[...] = one_hot((place // 4 == cj) & (column == cs))
+    rho = iota((NK, NK), 0)
+    rest = rho & (NS - 1)
+    slot = (rest & (n_pitch - 1)) * handoff + (rest // n_pitch) * 2 + rho // NS
+    slot_ref[...] = one_hot(slot == order_ref[...])
 
     mr, mc = iota((PAD, NS), 0), iota((PAD, NS), 1) & (PAD - 1)
     tr, tcol = (mr * 205) >> 10, (mc * 205) >> 10
@@ -340,6 +368,32 @@
     for t in range(NT):
         g_ref[t * NC : (t + 1) * NC, :] = g_part[t]
 
+    for copy in halos:
+        copy.wait_recv()
+    inner = jnp.concatenate([pitch_in[0, 1], pitch_in[1, 0]], axis=1)
+    high, low = split(inner)
+    mixed = dot(mix_p[...], jnp.concatenate([high, low, high, low], axis=0))
+    corr_ref[0] = -step_size * (
+        -0.5 * mixed[:, 0:NS] + damping * (pitch_in[0, 0] - 4.0 * pitch_in[0, 1])
+    )
+    corr_ref[1] = (-step_size * damping) * pitch_in[0, 1]
+    corr_ref[2] = (-step_size * damping) * pitch_in[1, 0]
+    corr_ref[3] = -step_size * (
+        0.5 * mixed[:, NS : 2 * NS] + damping * (pitch_in[1, 1] - 4.0 * pitch_in[1, 0])
+    )
+
+    high, low = split(corr_ref[0:4].reshape(4 * PAD, NS))
+    found = dot(jnp.concatenate([high, low], axis=1), cell_s[...])
+    total = g_ref[...]
+    for e, at_row in enumerate((0, 1, NJ - 2, NJ - 1)):
+        total = total + found[e * PAD : (e + 1) * PAD] * cell_j[at_row : at_row + 1, :]
+    g_ref[...] = total
+
+    @pl.when(below)
+    def _():
+        pl.semaphore_wait(answer, 1)
+        right.start()
+
     @pl.when(s < n_span - 1)
     def _():
         left_in = pltpu.make_async_copy(span_in.at[1], span_in.at[1], span_recv.at[1])
@@ -364,44 +418,32 @@
     mixed = dot(mix_s[...], jnp.concatenate([high, low, high, low], axis=0))
     corr_ref[4] = -step_size * (sign * mixed + damping * (x - 4.0 * y))
 
-    for copy in halos:
-        copy.wait_recv()
-    inner = jnp.concatenate([pitch_in[0, 1], pitch_in[1, 0]], axis=1)
-    high, low = split(inner)
-    mixed = dot(mix_p[...], jnp.concatenate([high, low, high, low], axis=0))
-    corr_ref[0] = -step_size * (
-        -0.5 * mixed[:, 0:NS] + damping * (pitch_in[0, 0] - 4.0 * pitch_in[0, 1])
-    )
-    corr_ref[1] = (-step_size * damping) * pitch_in[0, 1]
-    corr_ref[2] = (-step_size * damping) * pitch_in[1, 0]
-    corr_ref[3] = -step_size * (
-        0.5 * mixed[:, NS : 2 * NS] + damping * (pitch_in[1, 1] - 4.0 * pitch_in[1, 0])
-    )
-
     high, low = split(corr_ref[4])
     total = g_ref[...] + dot(jnp.concatenate([high, low], axis=1), cell_edge[...])
-    high, low = split(corr_ref[0:4].reshape(4 * PAD, NS))
-    found = dot(jnp.concatenate([high, low], axis=1), cell_s[...])
-    for e, at_row in enumerate((0, 1, NJ - 2, NJ - 1)):
-        total = total + found[e * PAD : (e + 1) * PAD] * cell_j[at_row : at_row + 1, :]
 
     turn_ref[...] = jnp.concatenate([total, pltpu.roll(total, NK - 1, 1)], axis=0).T
     for i in range(half):
         outgoing[:, i, :] = turn_ref[pl.ds(2 * i, n_pitch, stride=handoff), :]
 
+    line = min(8, n_pitch)
+
     def send(k, carry):
-        q = lax.rem(p + k, n_pitch)
-        pltpu.make_async_remote_copy(
-            outgoing.at[q],
-            arrived.at[p],
-            wall_send,
-            wall_recv,
-            device_id=(r, q, s),
-            device_id_type=MESH,
-        ).start()
+        q = (k % (n_pitch // line)) * line + k // (n_pitch // line)
+
+        @pl.when(q != p)
+        def _():
+            pltpu.make_async_remote_copy(
+                outgoing.at[q],
+                arrived.at[p],
+                wall_send,
+                wall_recv,
+                device_id=(r, q, s),
+                device_id_type=MESH,
+            ).start()
+
         return carry
 
-    lax.fori_loop(1, n_pitch, send, 0)
+    lax.fori_loop(0, n_pitch, send, 0)
     pltpu.make_async_copy(outgoing.at[p], arrived.at[p], wall_recv).start()
 
     for e, at_row in enumerate((0, 1, NJ - 2, NJ - 1)):
@@ -439,25 +481,18 @@
         left.wait_send()
 
 
-def finish(sizes, upd_ref, arrived, order_hbm, out_hbm, wall_ref, order_ref, sem):
-    n_pitch = sizes[1]
-    handoff = NK // n_pitch
-    load = pltpu.make_async_copy(order_hbm, order_ref, sem.at[0])
-    load.start()
+def finish(sizes, upd_ref, arrived, slot_ref, out_hbm, wall_ref, sem):
+    half = NK // sizes[1] // 2
     stores = []
     for i in range(PARTS):
         part = pl.ds(i * (ROWS // PARTS), ROWS // PARTS)
-        copy = pltpu.make_async_copy(upd_ref.at[part], out_hbm.at[part], sem.at[1 + i])
+        copy = pltpu.make_async_copy(upd_ref.at[part], out_hbm.at[part], sem.at[i])
         copy.start()
         stores.append(copy)
-    load.wait()
-
-    slots = jnp.concatenate([arrived[:, i, :] for i in range(handoff // 2)], axis=0).T
+
+    slots = jnp.concatenate([arrived[:, i, :] for i in range(half)], axis=0).T
     high, low = split(jnp.concatenate([slots[0:PAD], slots[PAD : 2 * PAD]], axis=1))
-    rho = iota((NK, NK), 0)
-    rest = rho & (NS - 1)
-    slot = (rest & (n_pitch - 1)) * handoff + (rest // n_pitch) * 2 + rho // NS
-    placed = dot(jnp.concatenate([high, low], axis=0), one_hot(slot == order_ref[...]))
+    placed = dot(jnp.concatenate([high, low], axis=0), slot_ref[...])
     placed = placed[0:PAD] + placed[PAD : 2 * PAD]
     for k in range(NK // NS):
         wall_ref[:, k, :] = placed[0:TC, k * NS : (k + 1) * NS]
@@ -472,11 +507,11 @@
     in_hbm = pl.BlockSpec(memory_space=pltpu.HBM)
     in_vmem = pl.BlockSpec(memory_space=pltpu.VMEM)
     smem = pltpu.SMEM
-    updated, arrived = pl.pallas_call(
+    updated, arrived, slots = pl.pallas_call(
         functools.partial(section, sizes),
-        out_shape=(vmem((ROWS, NS), F32), vmem((n_pitch, half, NS), F32)),
-        in_specs=[in_hbm] * 7,
-        out_specs=(in_vmem, in_vmem),
+        out_shape=(vmem((ROWS, NS), F32), vmem((n_pitch, half, NS), F32), vmem((NK, NK), BF16)),
+        in_specs=[in_hbm] * 8,
+        out_specs=(in_vmem, in_vmem, in_vmem),
         scratch_shapes=[
             smem((n_row,), I32),
             smem((n_row, H), I32),
@@ -488,6 +523,7 @@
             vmem((PAD, NC * NS), F32),
             vmem((4 * PAD, NC * NS), BF16),
             vmem((NT * NJ, 2 * NS), BF16),
+            vmem((1, NK), I32),
             vmem((1, NK), I32),
             vmem((2 * NS, NK), BF16),
             vmem((NJ, NK), F32),
@@ -504,7 +540,7 @@
             vmem((PAD, NK), F32),
             vmem((NK, NS), F32),
             vmem((n_pitch, half, NS), F32),
-            dma((6,)),
+            dma((PARTS + 6,)),
             dma((2,)),
             dma((2,)),
             dma((2,)),
@@ -513,6 +549,7 @@
             dma,
             dma,
             dma,
+            pltpu.SemaphoreType.REGULAR,
         ],
         compiler_params=pltpu.CompilerParams(
             collective_id=1, has_side_effects=True, vmem_limit_bytes=32 * 1024 * 1024
@@ -529,6 +566,7 @@
                 unknowns.reshape(ROWS, NS),
                 jnp.transpose(spectrum[0], (1, 2, 0, 3)).reshape(H * NC, 2, NS),
                 send_cell.reshape(1, NK),
+                recv_order.reshape(1, NK),
             )
         )
     )
@@ -538,19 +576,12 @@
             jax.ShapeDtypeStruct((ROWS, NS), F32),
             jax.ShapeDtypeStruct((TC, NK // NS, NS), F32),
         ),
-        in_specs=[in_vmem, in_vmem, in_hbm],
+        in_specs=[in_vmem] * 3,
         out_specs=(in_hbm, in_vmem),
-        scratch_shapes=[
-            vmem((1, NK), I32),
-            dma((1 + PARTS,)),
-        ],
+        scratch_shapes=[dma((PARTS,))],
         compiler_params=pltpu.CompilerParams(vmem_limit_bytes=8 * 1024 * 1024),
         name="wall_order",
-    )(
-        updated,
-        arrived,
-        pltpu.with_memory_space_constraint(recv_order.reshape(1, NK), pltpu.HBM),
-    )
+    )(updated, arrived, slots)
     return (
         updated.reshape(unknowns.shape),
         wall.reshape(1, 1, NT, NC, NK),

time: 43.6 us -> 40.1 us (0.920)
  Pallas kernels: 42.8 us -> 39.3 us
    pallas_call x1, Pallas kernels: 41.2 us -> 37.7 us  [local(): pl.pallas_call(functools.partial(section, sizes), out_shape=(vmem((ROWS,...]
where the time goes in v3:
time: 40.1 us; the launch traced here: 40 us
  Pallas kernels  39.3 us (98%)
  between operations  0.64 us (2%)
    pallas_call x1, Pallas kernels, local(): pl.pallas_call(functools.partial(section, sizes), out_shape=(vmem((ROWS,...  37.7 us
    pallas_call x1, Pallas kernels, local(): pl.pallas_call(functools.partial(finish, sizes), out_shape=(jax.ShapeDtyp...  1.62 us

profile of v3, /device:TPU:1, one launch (start us, length us, event | category | flops | bytes accessed | tf_op | source)
XLA Modules:
  0.0 40.0 jit_solution(14944330260948118762)
XLA Ops:
  0.6 37.7 %flux_section.1 = (f32[1760,128]{1,0:T(8,128)S(1)}, f32[64,2,128]{2,1,0:T(2,128)S(1)}, bf16[256,256]{1,0:T(8,128)(2,1)S(1)}) custom-call(s32[4]{0:T(128)} %blades_hbm.1, s32[4,5]{1,0:T(4,128)} %harmonics_hbm.1, f32[5,5]{1,0:T(8,128)} %pitch_jac_hbm.1, f32[5,5]{1,0:T(8,128)} %span_jac_hbm.1, f32[1760,128]{1,0:T(8,128)} %bitcast.10, f32[25,2,128]{2,1,0:T(2,128)} %bitcast.11, ...), custom_call_target="tpu_custom_call" | custom-call | tf_op jit(solution)/shard_map/flux_section/pallas_call | solution.py:510
  38.3 1.6 %wall_order.1 = (f32[1760,128]{1,0:T(8,128)}, f32[55,2,128]{2,1,0:T(2,128)}) custom-call(f32[1760,128]{1,0:T(8,128)S(1)} %get-tuple-element.7.upd_ref, f32[64,2,128]{2,1,0:T(2,128)S(1)} %get-tuple-element.8.arrived, bf16[256,256]{1,0:T(8,128)(2,1)S(1)} %get-tuple-element.9.slot_ref), custom_call_target="tpu_custom_call" | custom-call | tf_op jit(solution)/shard_map/wall_order/pallas_call | solution.py:573

commit v4 on v3

--- a/solution.py
+++ b/solution.py
@@ -109,7 +109,7 @@
     r, p, s = lax.axis_index("row"), lax.axis_index("pitch"), lax.axis_index("span")
 
     def pitch_peer(k):
-        return (r, lax.rem(p + k, n_pitch), s)
+        return (r, (p + k) & (n_pitch - 1), s)
 
     def row_peer(k):
         return (lax.rem(r + k, n_row), p, s)
@@ -140,11 +140,55 @@
     for k in range(1, n_row):
         pl.semaphore_signal(barrier, inc=1, device_id=row_peer(k), device_id_type=MESH)
 
-    def greet(k, carry):
+    for k in range(2, n_pitch - 1):
         pl.semaphore_signal(barrier, inc=1, device_id=pitch_peer(k), device_id_type=MESH)
-        return carry
-
-    lax.fori_loop(2, n_pitch - 1, greet, 0)
+
+    lane = iota((1, NS), 1)
+
+    for copy in loads:
+        copy.wait()
+    edges = jnp.zeros((TC, NS), F32)
+    for j in range(NJ):
+        turned = pltpu.roll(u_ref[pl.ds(j, TC, stride=NJ), :], (2 + 4 * j) % NS, 1)
+        edges = jnp.where((lane >= 4 * j) & (lane < 4 * j + 4), turned, edges)
+    edge_ref[0:TC, :] = edges
+    edge_ref[TC:PAD, :] = jnp.zeros((PAD - TC, NS), F32)
+    e4 = lax.rem(lane, 4)
+    low, high = edge_ref[0 : PAD // 2, :], edge_ref[PAD // 2 : PAD, :]
+    span_out[0] = jnp.where(e4 < 2, low, pltpu.roll(high, 2, 1))
+    span_out[1] = jnp.where(e4 >= 2, low, pltpu.roll(high, NS - 2, 1))
+
+    greeters = 1 + n_row - 1 + n_pitch - 1
+    pl.semaphore_wait(barrier, jnp.where(above, greeters + 1, greeters))
+
+    @pl.when(above)
+    def _():
+        pl.semaphore_signal(answer, inc=1, device_id=span_peer(-1), device_id_type=MESH)
+
+    right = pltpu.make_async_remote_copy(
+        span_out.at[0],
+        span_in.at[0],
+        span_send.at[0],
+        span_recv.at[0],
+        device_id=span_peer(1),
+        device_id_type=MESH,
+    )
+    left = pltpu.make_async_remote_copy(
+        span_out.at[1],
+        span_in.at[1],
+        span_send.at[1],
+        span_recv.at[1],
+        device_id=span_peer(-1),
+        device_id_type=MESH,
+    )
+
+    @pl.when(s > 0)
+    def _():
+        left.start()
+
+    @pl.when((s < n_span - 1) & (s != middle - 1))
+    def _():
+        right.start()
 
     scalars = []
     for i, (src, dst) in enumerate(
@@ -160,53 +204,6 @@
         copy = pltpu.make_async_copy(src, dst, load_sem.at[PARTS + i])
         copy.start()
         scalars.append(copy)
-
-    lane = iota((1, NS), 1)
-
-    for copy in loads:
-        copy.wait()
-    edges = jnp.zeros((TC, NS), F32)
-    for j in range(NJ):
-        turned = pltpu.roll(u_ref[pl.ds(j, TC, stride=NJ), :], (2 + 4 * j) % NS, 1)
-        edges = jnp.where((lane >= 4 * j) & (lane < 4 * j + 4), turned, edges)
-    edge_ref[0:TC, :] = edges
-    edge_ref[TC:PAD, :] = jnp.zeros((PAD - TC, NS), F32)
-    e4 = lax.rem(lane, 4)
-    low, high = edge_ref[0 : PAD // 2, :], edge_ref[PAD // 2 : PAD, :]
-    span_out[0] = jnp.where(e4 < 2, low, pltpu.roll(high, 2, 1))
-    span_out[1] = jnp.where(e4 >= 2, low, pltpu.roll(high, NS - 2, 1))
-
-    greeters = 1 + n_row - 1 + n_pitch - 1
-    pl.semaphore_wait(barrier, jnp.where(above, greeters + 1, greeters))
-
-    @pl.when(above)
-    def _():
-        pl.semaphore_signal(answer, inc=1, device_id=span_peer(-1), device_id_type=MESH)
-
-    right = pltpu.make_async_remote_copy(
-        span_out.at[0],
-        span_in.at[0],
-        span_send.at[0],
-        span_recv.at[0],
-        device_id=span_peer(1),
-        device_id_type=MESH,
-    )
-    left = pltpu.make_async_remote_copy(
-        span_out.at[1],
-        span_in.at[1],
-        span_send.at[1],
-        span_recv.at[1],
-        device_id=span_peer(-1),
-        device_id_type=MESH,
-    )
-
-    @pl.when(s > 0)
-    def _():
-        left.start()
-
-    @pl.when((s < n_span - 1) & (s != middle - 1))
-    def _():
-        right.start()
 
     pitch_out[:, :, TC:PAD, :] = jnp.zeros((2, 2, PAD - TC, NS), F32)
     for layer in range(2):
@@ -427,23 +424,24 @@
 
     line = min(8, n_pitch)
 
-    def send(k, carry):
-        q = (k % (n_pitch // line)) * line + k // (n_pitch // line)
-
-        @pl.when(q != p)
-        def _():
-            pltpu.make_async_remote_copy(
-                outgoing.at[q],
-                arrived.at[p],
-                wall_send,
-                wall_recv,
-                device_id=(r, q, s),
-                device_id_type=MESH,
-            ).start()
+    def send(z, carry):
+        for y in range(n_pitch // line):
+            q = y * line + z
+
+            @pl.when(q != p)
+            def _():
+                pltpu.make_async_remote_copy(
+                    outgoing.at[q],
+                    arrived.at[p],
+                    wall_send,
+                    wall_recv,
+                    device_id=(r, q, s),
+                    device_id_type=MESH,
+                ).start()
 
         return carry
 
-    lax.fori_loop(0, n_pitch, send, 0)
+    lax.fori_loop(0, line, send, 0)
     pltpu.make_async_copy(outgoing.at[p], arrived.at[p], wall_recv).start()
 
     for e, at_row in enumerate((0, 1, NJ - 2, NJ - 1)):

time: 40.1 us -> 40.3 us (level)
  no operation moved by 1% of the time
where the time goes in v4:
time: 40.3 us; the launch traced here: 40.1 us
  Pallas kernels  39.5 us (98%)
  between operations  0.64 us (2%)
    pallas_call x1, Pallas kernels, local(): pl.pallas_call(functools.partial(section, sizes), out_shape=(vmem((ROWS,...  37.9 us
    pallas_call x1, Pallas kernels, local(): pl.pallas_call(functools.partial(finish, sizes), out_shape=(jax.ShapeDtyp...  1.62 us

profile of v4, /device:TPU:1, one launch (start us, length us, event | category | flops | bytes accessed | tf_op | source)
XLA Modules:
  0.0 40.1 jit_solution(1866362884872247605)
XLA Ops:
  0.6 37.9 %flux_section.1 = (f32[1760,128]{1,0:T(8,128)S(1)}, f32[64,2,128]{2,1,0:T(2,128)S(1)}, bf16[256,256]{1,0:T(8,128)(2,1)S(1)}) custom-call(s32[4]{0:T(128)} %blades_hbm.1, s32[4,5]{1,0:T(4,128)} %harmonics_hbm.1, f32[5,5]{1,0:T(8,128)} %pitch_jac_hbm.1, f32[5,5]{1,0:T(8,128)} %span_jac_hbm.1, f32[1760,128]{1,0:T(8,128)} %bitcast.10, f32[25,2,128]{2,1,0:T(2,128)} %bitcast.11, ...), custom_call_target="tpu_custom_call" | custom-call | tf_op jit(solution)/shard_map/flux_section/pallas_call | solution.py:508
  38.5 1.6 %wall_order.1 = (f32[1760,128]{1,0:T(8,128)}, f32[55,2,128]{2,1,0:T(2,128)}) custom-call(f32[1760,128]{1,0:T(8,128)S(1)} %get-tuple-element.7.upd_ref, f32[64,2,128]{2,1,0:T(2,128)S(1)} %get-tuple-element.8.arrived, bf16[256,256]{1,0:T(8,128)(2,1)S(1)} %get-tuple-element.9.slot_ref), custom_call_target="tpu_custom_call" | custom-call | tf_op jit(solution)/shard_map/wall_order/pallas_call | solution.py:571

commit v5 on v3

--- a/solution.py
+++ b/solution.py
@@ -223,8 +223,13 @@
             device_id=pitch_peer(k),
             device_id_type=MESH,
         )
-        copy.start()
         halos.append(copy)
+
+    @pl.when(s < middle)
+    def _():
+        for copy in halos:
+            copy.start()
+
     spectra = []
     for k in range(1, n_row):
         copy = pltpu.make_async_remote_copy(
@@ -339,6 +344,12 @@
         return carry
 
     lax.fori_loop(0, NT, interior, 0)
+
+    @pl.when(s >= middle)
+    def _():
+        for copy in halos:
+            copy.start()
+
 
     pltpu.make_async_copy(specs, specs, row_recv).wait()
     for g in range(n_row):

time: 40.1 us -> 40.1 us (level)
  no operation moved by 1% of the time
where the time goes in v5:
time: 40.1 us; the launch traced here: 39.8 us
  Pallas kernels  39.1 us (98%)
  between operations  0.64 us (2%)
    pallas_call x1, Pallas kernels, local(): pl.pallas_call(functools.partial(section, sizes), out_shape=(vmem((ROWS,...  37.5 us
    pallas_call x1, Pallas kernels, local(): pl.pallas_call(functools.partial(finish, sizes), out_shape=(jax.ShapeDtyp...  1.62 us

profile of v5, /device:TPU:1, one launch (start us, length us, event | category | flops | bytes accessed | tf_op | source)
XLA Modules:
  0.0 39.8 jit_solution(1534941250894836636)
XLA Ops:
  0.6 37.5 %flux_section.1 = (f32[1760,128]{1,0:T(8,128)S(1)}, f32[64,2,128]{2,1,0:T(2,128)S(1)}, bf16[256,256]{1,0:T(8,128)(2,1)S(1)}) custom-call(s32[4]{0:T(128)} %blades_hbm.1, s32[4,5]{1,0:T(4,128)} %harmonics_hbm.1, f32[5,5]{1,0:T(8,128)} %pitch_jac_hbm.1, f32[5,5]{1,0:T(8,128)} %span_jac_hbm.1, f32[1760,128]{1,0:T(8,128)} %bitcast.10, f32[25,2,128]{2,1,0:T(2,128)} %bitcast.11, ...), custom_call_target="tpu_custom_call" | custom-call | tf_op jit(solution)/shard_map/flux_section/pallas_call | solution.py:521
  38.2 1.6 %wall_order.1 = (f32[1760,128]{1,0:T(8,128)}, f32[55,2,128]{2,1,0:T(2,128)}) custom-call(f32[1760,128]{1,0:T(8,128)S(1)} %get-tuple-element.7.upd_ref, f32[64,2,128]{2,1,0:T(2,128)S(1)} %get-tuple-element.8.arrived, bf16[256,256]{1,0:T(8,128)(2,1)S(1)} %get-tuple-element.9.slot_ref), custom_call_target="tpu_custom_call" | custom-call | tf_op jit(solution)/shard_map/wall_order/pallas_call | solution.py:584

commit v6 on v5

--- a/solution.py
+++ b/solution.py
@@ -146,6 +146,53 @@
 
     lax.fori_loop(2, n_pitch - 1, greet, 0)
 
+    lane = iota((1, NS), 1)
+
+    for copy in loads:
+        copy.wait()
+    edges = jnp.zeros((TC, NS), F32)
+    for j in range(NJ):
+        turned = pltpu.roll(u_ref[pl.ds(j, TC, stride=NJ), :], (2 + 4 * j) % NS, 1)
+        edges = jnp.where((lane >= 4 * j) & (lane < 4 * j + 4), turned, edges)
+    edge_ref[0:TC, :] = edges
+    edge_ref[TC:PAD, :] = jnp.zeros((PAD - TC, NS), F32)
+    e4 = lax.rem(lane, 4)
+    low, high = edge_ref[0 : PAD // 2, :], edge_ref[PAD // 2 : PAD, :]
+    span_out[0] = jnp.where(e4 < 2, low, pltpu.roll(high, 2, 1))
+    span_out[1] = jnp.where(e4 >= 2, low, pltpu.roll(high, NS - 2, 1))
+
+    greeters = 1 + n_row - 1 + n_pitch - 1
+    pl.semaphore_wait(barrier, jnp.where(above, greeters + 1, greeters))
+
+    @pl.when(above)
+    def _():
+        pl.semaphore_signal(answer, inc=1, device_id=span_peer(-1), device_id_type=MESH)
+
+    right = pltpu.make_async_remote_copy(
+        span_out.at[0],
+        span_in.at[0],
+        span_send.at[0],
+        span_recv.at[0],
+        device_id=span_peer(1),
+        device_id_type=MESH,
+    )
+    left = pltpu.make_async_remote_copy(
+        span_out.at[1],
+        span_in.at[1],
+        span_send.at[1],
+        span_recv.at[1],
+        device_id=span_peer(-1),
+        device_id_type=MESH,
+    )
+
+    @pl.when(s > 0)
+    def _():
+        left.start()
+
+    @pl.when((s < n_span - 1) & (s != middle - 1))
+    def _():
+        right.start()
+
     scalars = []
     for i, (src, dst) in enumerate(
         (
@@ -160,53 +207,6 @@
         copy = pltpu.make_async_copy(src, dst, load_sem.at[PARTS + i])
         copy.start()
         scalars.append(copy)
-
-    lane = iota((1, NS), 1)
-
-    for copy in loads:
-        copy.wait()
-    edges = jnp.zeros((TC, NS), F32)
-    for j in range(NJ):
-        turned = pltpu.roll(u_ref[pl.ds(j, TC, stride=NJ), :], (2 + 4 * j) % NS, 1)
-        edges = jnp.where((lane >= 4 * j) & (lane < 4 * j + 4), turned, edges)
-    edge_ref[0:TC, :] = edges
-    edge_ref[TC:PAD, :] = jnp.zeros((PAD - TC, NS), F32)
-    e4 = lax.rem(lane, 4)
-    low, high = edge_ref[0 : PAD // 2, :], edge_ref[PAD // 2 : PAD, :]
-    span_out[0] = jnp.where(e4 < 2, low, pltpu.roll(high, 2, 1))
-    span_out[1] = jnp.where(e4 >= 2, low, pltpu.roll(high, NS - 2, 1))
-
-    greeters = 1 + n_row - 1 + n_pitch - 1
-    pl.semaphore_wait(barrier, jnp.where(above, greeters + 1, greeters))
-
-    @pl.when(above)
-    def _():
-        pl.semaphore_signal(answer, inc=1, device_id=span_peer(-1), device_id_type=MESH)
-
-    right = pltpu.make_async_remote_copy(
-        span_out.at[0],
-        span_in.at[0],
-        span_send.at[0],
-        span_recv.at[0],
-        device_id=span_peer(1),
-        device_id_type=MESH,
-    )
-    left = pltpu.make_async_remote_copy(
-        span_out.at[1],
-        span_in.at[1],
-        span_send.at[1],
-        span_recv.at[1],
-        device_id=span_peer(-1),
-        device_id_type=MESH,
-    )
-
-    @pl.when(s > 0)
-    def _():
-        left.start()
-
-    @pl.when((s < n_span - 1) & (s != middle - 1))
-    def _():
-        right.start()
 
     pitch_out[:, :, TC:PAD, :] = jnp.zeros((2, 2, PAD - TC, NS), F32)
     for layer in range(2):
@@ -345,12 +345,6 @@
 
     lax.fori_loop(0, NT, interior, 0)
 
-    @pl.when(s >= middle)
-    def _():
-        for copy in halos:
-            copy.start()
-
-
     pltpu.make_async_copy(specs, specs, row_recv).wait()
     for g in range(n_row):
         for n in range(H):
@@ -376,6 +370,12 @@
         return carry
 
     lax.fori_loop(0, NT, gather, 0)
+
+    @pl.when(s >= middle)
+    def _():
+        for copy in halos:
+            copy.start()
+
     for t in range(NT):
         g_ref[t * NC : (t + 1) * NC, :] = g_part[t]
 

time: 40.1 us -> 40.4 us (level)
  no operation moved by 1% of the time
where the time goes in v6:
time: 40.4 us; the launch traced here: 39.8 us
  Pallas kernels  39.1 us (97%)
  between operations  0.64 us (2%)
    pallas_call x1, Pallas kernels, local(): pl.pallas_call(functools.partial(section, sizes), out_shape=(vmem((ROWS,...  37.5 us
    pallas_call x1, Pallas kernels, local(): pl.pallas_call(functools.partial(finish, sizes), out_shape=(jax.ShapeDtyp...  1.62 us

profile of v6, /device:TPU:1, one launch (start us, length us, event | category | flops | bytes accessed | tf_op | source)
XLA Modules:
  0.0 39.8 jit_solution(9965649812242414917)
XLA Ops:
  0.6 37.5 %flux_section.1 = (f32[1760,128]{1,0:T(8,128)S(1)}, f32[64,2,128]{2,1,0:T(2,128)S(1)}, bf16[256,256]{1,0:T(8,128)(2,1)S(1)}) custom-call(s32[4]{0:T(128)} %blades_hbm.1, s32[4,5]{1,0:T(4,128)} %harmonics_hbm.1, f32[5,5]{1,0:T(8,128)} %pitch_jac_hbm.1, f32[5,5]{1,0:T(8,128)} %span_jac_hbm.1, f32[1760,128]{1,0:T(8,128)} %bitcast.10, f32[25,2,128]{2,1,0:T(2,128)} %bitcast.11, ...), custom_call_target="tpu_custom_call" | custom-call | tf_op jit(solution)/shard_map/flux_section/pallas_call | solution.py:521
  38.2 1.6 %wall_order.1 = (f32[1760,128]{1,0:T(8,128)}, f32[55,2,128]{2,1,0:T(2,128)}) custom-call(f32[1760,128]{1,0:T(8,128)S(1)} %get-tuple-element.7.upd_ref, f32[64,2,128]{2,1,0:T(2,128)S(1)} %get-tuple-element.8.arrived, bf16[256,256]{1,0:T(8,128)(2,1)S(1)} %get-tuple-element.9.slot_ref), custom_call_target="tpu_custom_call" | custom-call | tf_op jit(solution)/shard_map/wall_order/pallas_call | solution.py:584
